TPU v7x, 256 devices: a whole 4x4x8 slice. The times are simulated.
256 devices in a mesh: seq: 32 (over z_lo, x, core), head: 8 (over y, z_hi).
Axes of the slice: x: 4, y: 4, z: 8 (z_hi: 2, z_lo: 4; z = z_hi * 4 + z_lo), core: 2. Of those that a mesh axis runs over, the one named last changes fastest.
Arguments:
- activations: bfloat16 [16384, 4096], P('seq'), may hold values from -400 to 400
- norm_gain: float32 [4096], replicated, may hold values from 0.1 to 1.9
- shifted: int32 [16], replicated, may hold values from 0 to 1, as said below
- query_weight: bfloat16 [4096, 2048], P('seq', 'head'), may hold values from -0.1875 to 0.1875
- key_weight: bfloat16 [4096, 2048], P('seq', 'head'), may hold values from -0.1875 to 0.1875
- value_weight: bfloat16 [4096, 2048], P('seq', 'head'), may hold values from -0.09375 to 0.09375
- output_weight: bfloat16 [2048, 4096], P('head', 'seq'), may hold values from -0.25 to 0.25
- query_down: bfloat16 [4096, 64], replicated, may hold values from -0.09375 to 0.09375
- query_up: bfloat16 [64, 2048], replicated, may hold values from -0.75 to 0.75
- key_down: bfloat16 [4096, 64], replicated, may hold values from -0.09375 to 0.09375
- key_up: bfloat16 [64, 2048], replicated, may hold values from -0.75 to 0.75
- value_down: bfloat16 [4096, 64], replicated, may hold values from -0.09375 to 0.09375
- value_up: bfloat16 [64, 2048], replicated, may hold values from -0.75 to 0.75
- output_down: bfloat16 [2048, 64], replicated, may hold values from -0.125 to 0.125
- output_up_matrix: bfloat16 [64, 4096], replicated, may hold values from -0.75 to 0.75
Outputs:
- attended: bfloat16 [16384, 4096], P('seq', 'head')
- log_sums: float32 [16384, 16], P('seq', 'head')
Inputs may be any that keep to these rules, and one draw needn't show every extreme that they name: Exactly 8 heads are shifted; which ones is drawn.
All inputs are finite; a program needn't handle non-finite values.
Results may differ from a plain program's by a relative error of at most 0.02.
Values may be sent and summed in bfloat16 or wider, within the bound.
A program may use at most 64 MiB of HBM per device.

v0:
```python
import math

import jax
import jax.numpy as jnp
from jax import lax
from jax.sharding import PartitionSpec as P

HD = 128
GROUP_DEV = 16


EPS = 1e-05
ADAPTER_SCALING = 0.5
ROPE_BASE = 10000.0
MASKED = -1e30


def from_behind(value, axis, steps):
    count = lax.axis_size(axis)
    pairs = [(source, (source + steps) % count) for source in range(count)]
    return lax.ppermute(value, axis, pairs)


def normalize(values, gain):
    widened = values.astype(jnp.float32)
    mean_square = jnp.mean(widened * widened, axis=-1, keepdims=True)
    return (widened * lax.rsqrt(mean_square + EPS) * gain).astype(jnp.bfloat16)


def rotate(values, positions, head_size):
    halfway = head_size // 2
    frequency = ROPE_BASE ** (-2.0 * jnp.arange(halfway).astype(jnp.float32) / head_size)
    angles = positions.astype(jnp.float32)[:, None] * frequency[None, :]
    cosine = jnp.cos(angles)[:, None, :]
    sine = jnp.sin(angles)[:, None, :]
    shaped = values.reshape(values.shape[0], -1, head_size)
    leading = shaped[..., :halfway]
    trailing = shaped[..., halfway:]
    turned = jnp.concatenate(
        [leading * cosine - trailing * sine, trailing * cosine + leading * sine], axis=-1
    )
    return turned.reshape(values.shape).astype(jnp.bfloat16)


def key_blocks(state, stacked, key_pos, query_heads, query_rel, offsets, group_len, seq_len):
    length = stacked.shape[1]
    count = length // length
    heads_here = query_heads.shape[0]
    head_size = query_heads.shape[2]
    key_tiles = stacked[0].reshape(count, length, heads_here, head_size)
    value_tiles = stacked[1].reshape(count, length, heads_here, head_size)
    position_tiles = key_pos.reshape(count, length)
    scale = 1.0 / math.sqrt(head_size)

    def one_block(running, tiles):
        running_max, running_sum, running_acc = running
        key_tile, value_tile, position_tile = tiles
        key_rel = (position_tile[None, :] - offsets[:, None] + seq_len) % seq_len
        allowed = (query_rel[:, :, None] // group_len == key_rel[:, None, :] // group_len) & (
            key_rel[:, None, :] <= query_rel[:, :, None]
        )
        scores = (
            jnp.einsum("hqd,khd->hqk", query_heads, key_tile, preferred_element_type=jnp.float32)
            * scale
        )
        scores = jnp.where(allowed, scores, MASKED)
        new_max = jnp.maximum(running_max, jnp.max(scores, axis=2))
        weights = jnp.where(allowed, jnp.exp(scores - new_max[:, :, None]), 0.0)
        rescale = jnp.exp(running_max - new_max)
        new_sum = running_sum * rescale + jnp.sum(weights, axis=2)
        update = jnp.einsum(
            "hqk,khd->hqd",
            weights.astype(jnp.bfloat16),
            value_tile,
            preferred_element_type=jnp.float32,
        )
        new_acc = running_acc * rescale[:, :, None] + update
        return ((new_max, new_sum, new_acc), None)

    finished, unused = lax.scan(one_block, state, (key_tiles, value_tiles, position_tiles))
    return finished


def body(
    activations,
    norm_gain,
    shifted,
    query_weight,
    key_weight,
    value_weight,
    output_weight,
    query_down,
    query_up,
    key_down,
    key_up,
    value_down,
    value_up,
    output_down,
    output_up_matrix,
):
    rows = activations.shape[0]
    local_width = query_weight.shape[1]
    head_size = HD
    heads_here = local_width // head_size
    head_index = lax.axis_index("head")
    seq_index = lax.axis_index("seq")
    seq_devices = lax.axis_size("seq")
    seq_len = rows * seq_devices
    group_len = rows * GROUP_DEV
    normed = normalize(activations, norm_gain)
    pieces = (
        lax.all_gather(query_weight, "seq", axis=0, tiled=True),
        lax.all_gather(key_weight, "seq", axis=0, tiled=True),
        lax.all_gather(value_weight, "seq", axis=0, tiled=True),
    )
    query_direct, key_direct, value_direct = tuple(
        (jnp.dot(normed, piece, preferred_element_type=jnp.float32) for piece in pieces)
    )

    def low_rank(down_factor, up_projection_factor):
        up_factor_columns = lax.dynamic_slice_in_dim(
            up_projection_factor, head_index * local_width, local_width, 1
        )
        reduced_result = jnp.dot(normed, down_factor, preferred_element_type=jnp.float32).astype(
            jnp.bfloat16
        )
        return ADAPTER_SCALING * jnp.dot(
            reduced_result, up_factor_columns, preferred_element_type=jnp.float32
        )

    positions = seq_index * rows + jnp.arange(rows, dtype=jnp.int32)
    queries = rotate(query_direct + low_rank(query_down, query_up), positions, head_size)
    keys_here = rotate(key_direct + low_rank(key_down, key_up), positions, head_size)
    values_here = (value_direct + low_rank(value_down, value_up)).astype(jnp.bfloat16)
    flags = lax.dynamic_slice_in_dim(shifted, head_index * heads_here, heads_here, 0)
    offsets = flags * (group_len // 2)
    query_heads = queries.reshape(rows, heads_here, head_size).transpose(1, 0, 2)
    query_rel = (positions[None, :] - offsets[:, None] + seq_len) % seq_len
    stacked = jnp.stack([keys_here, values_here])
    start_state = (
        jnp.full((heads_here, rows), MASKED, jnp.float32),
        jnp.zeros((heads_here, rows), jnp.float32),
        jnp.zeros((heads_here, rows, head_size), jnp.float32),
    )
    own_state = key_blocks(
        start_state, stacked, positions, query_heads, query_rel, offsets, group_len, seq_len
    )

    def one_step(step, carried):
        piece, running = carried
        arrived = from_behind(piece, "seq", 1)
        slab = (seq_index - step + seq_devices) % seq_devices
        piece_pos = slab * rows + jnp.arange(rows, dtype=jnp.int32)
        return (
            arrived,
            key_blocks(
                running, arrived, piece_pos, query_heads, query_rel, offsets, group_len, seq_len
            ),
        )

    unused_piece, final_state = lax.fori_loop(1, GROUP_DEV, one_step, (stacked, own_state))
    final_max, final_sum, final_acc = final_state
    mixed = (
        (final_acc / final_sum[:, :, None])
        .transpose(1, 0, 2)
        .reshape(rows, local_width)
        .astype(jnp.bfloat16)
    )
    log_sums = (final_max + jnp.log(final_sum)).T
    down_rows = lax.dynamic_slice_in_dim(output_down, head_index * local_width, local_width, 0)
    reduced_result = jnp.dot(mixed, down_rows, preferred_element_type=jnp.float32).astype(
        jnp.bfloat16
    )
    up_factor_columns = output_up_matrix
    direct_path = jnp.dot(
        mixed,
        lax.all_gather(output_weight, "seq", axis=1, tiled=True),
        preferred_element_type=jnp.float32,
    )
    summand_terms = direct_path + ADAPTER_SCALING * jnp.dot(
        reduced_result, up_factor_columns, preferred_element_type=jnp.float32
    )
    summed = lax.psum_scatter(
        summand_terms.astype(jnp.bfloat16), "head", scatter_dimension=1, tiled=True
    )
    return (summed, log_sums)


def solution(mesh):
    placed = (
        P("seq", None),
        P(),
        P(),
        P("seq", "head"),
        P("seq", "head"),
        P("seq", "head"),
        P("head", "seq"),
        P(),
        P(),
        P(),
        P(),
        P(),
        P(),
        P(),
        P(),
    )
    return jax.shard_map(
        body,
        mesh=mesh,
        in_specs=placed,
        out_specs=(P("seq", "head"), P("seq", "head")),
        check_vma=False,
    )
```

profile of v0, /device:TPU:38, one launch (start us, length us, event | category | flops | bytes accessed | tf_op | source)
XLA Modules:
  0.0 611.2 jit_solution(8357241788165143050)
XLA Ops:
  10.1 3.1 fusion.25
  14.4 5.8 fusion.27
  20.1 50.9 %all-gather.5.cloned.1.call-done = bf16[4096,256]{1,0:T(8,128)(2,1)} async-done(((bf16[128,256]{1,0:T(8,128)(2,1)}), bf16[4096,256]{1,0:T(8,128)(2,1)}) %all-gather.5.cloned.1.call-update) | async-done | bytes 2097168 | tf_op jit(solution)/shard_map/all_gather | solution.py:113
  71.0 4.2 fusion.56
  75.2 3.7 fusion.29
  79.0 53.0 %all-gather.9.cloned.1.call-done = bf16[4096,256]{1,0:T(8,128)(2,1)} async-done(((bf16[128,256]{1,0:T(8,128)(2,1)}), bf16[4096,256]{1,0:T(8,128)(2,1)}) %all-gather.9.cloned.1.call-update) | async-done | bytes 2097168 | tf_op jit(solution)/shard_map/all_gather | solution.py:112
  132.0 4.2 fusion.58
  136.2 3.7 fusion.31
  143.4 49.6 %all-gather.7.cloned.1.call-done = bf16[4096,256]{1,0:T(8,128)(2,1)} async-done(((bf16[128,256]{1,0:T(8,128)(2,1)}), bf16[4096,256]{1,0:T(8,128)(2,1)}) %all-gather.7.cloned.1.call-update) | async-done | bytes 2097168 | tf_op jit(solution)/shard_map/all_gather | solution.py:114
  192.9 5.0 fusion.57
  197.9 4.0 fusion.32
  204.9 217.2 %while.44 = (s32[]{:T(128)}, bf16[2,512,256]{1,2,0:T(8,128)(2,1)}, f32[2,512]{1,0:T(2,128)S(1)}, f32[2,512]{1,0:T(2,128)S(1)}, f32[2,512,128]{2,1,0:T(8,128)}, /...) while((s32[]{:T(128)}, bf16[2,512,256]{1,2,0:T(8,128)(2,1)}, ...), condition=%wide.region_6.7_spmd.clone.clone, body=%wide.region_3.6_spmd.clone.clone.sunk | while | flops 280305152 | bytes 16652674 | solution.py:161
  205.2 10.2 %collective-permute-done = bf16[2,512,256]{1,2,0:T(8,128)(2,1)S(1)} collective-permute-done((bf16[2,512,256]{1,2,0:T(8,128)(2,1)}, bf16[2,512,256]{1,2,0:T(8,128)(2,1)S(1)}, u32[]{:S(2)}, u32[]{:S(2)}) %collective-permute-start) | collective-permute-done | bytes 524320 | tf_op jit(solution)/shard_map/while/body/eval_jaxpr/ppermute | solution.py:21
  219.9 9.4 %collective-permute-done = bf16[2,512,256]{1,2,0:T(8,128)(2,1)S(1)} collective-permute-done((bf16[2,512,256]{1,2,0:T(8,128)(2,1)}, bf16[2,512,256]{1,2,0:T(8,128)(2,1)S(1)}, u32[]{:S(2)}, u32[]{:S(2)}) %collective-permute-start) | collective-permute-done | bytes 524320 | tf_op jit(solution)/shard_map/while/body/eval_jaxpr/ppermute | solution.py:21
  233.8 10.4 %collective-permute-done = bf16[2,512,256]{1,2,0:T(8,128)(2,1)S(1)} collective-permute-done((bf16[2,512,256]{1,2,0:T(8,128)(2,1)}, bf16[2,512,256]{1,2,0:T(8,128)(2,1)S(1)}, u32[]{:S(2)}, u32[]{:S(2)}) %collective-permute-start) | collective-permute-done | bytes 524320 | tf_op jit(solution)/shard_map/while/body/eval_jaxpr/ppermute | solution.py:21
  248.7 9.4 %collective-permute-done = bf16[2,512,256]{1,2,0:T(8,128)(2,1)S(1)} collective-permute-done((bf16[2,512,256]{1,2,0:T(8,128)(2,1)}, bf16[2,512,256]{1,2,0:T(8,128)(2,1)S(1)}, u32[]{:S(2)}, u32[]{:S(2)}) %collective-permute-start) | collective-permute-done | bytes 524320 | tf_op jit(solution)/shard_map/while/body/eval_jaxpr/ppermute | solution.py:21
  263.6 7.6 %collective-permute-done = bf16[2,512,256]{1,2,0:T(8,128)(2,1)S(1)} collective-permute-done((bf16[2,512,256]{1,2,0:T(8,128)(2,1)}, bf16[2,512,256]{1,2,0:T(8,128)(2,1)S(1)}, u32[]{:S(2)}, u32[]{:S(2)}) %collective-permute-start) | collective-permute-done | bytes 524320 | tf_op jit(solution)/shard_map/while/body/eval_jaxpr/ppermute | solution.py:21
  275.5 3.2 collective-permute-start
  278.9 5.5 collective-permute-done
  288.7 5.3 collective-permute-start
  294.1 3.4 collective-permute-done
  301.8 7.4 %collective-permute-start = (bf16[2,512,256]{1,2,0:T(8,128)(2,1)}, bf16[2,512,256]{1,2,0:T(8,128)(2,1)S(1)}, u32[]{:S(2)}, u32[]{:S(2)}) collective-permute-start(bf16[2,512,256]{1,2,0:T(8,128)(2,1)} %get-tuple-element.572), channel_id=1, source_target_pairs={{0,8},{8,16},{16,24},{24,32},{32,40},{40,48},{48,56},{56,64},{64,7... | collective-permute-start | bytes 1572872 | tf_op jit(solution)/shard_map/while/body/eval_jaxpr/ppermute | solution.py:21
  315.3 9.2 %collective-permute-start = (bf16[2,512,256]{1,2,0:T(8,128)(2,1)}, bf16[2,512,256]{1,2,0:T(8,128)(2,1)S(1)}, u32[]{:S(2)}, u32[]{:S(2)}) collective-permute-start(bf16[2,512,256]{1,2,0:T(8,128)(2,1)} %get-tuple-element.572), channel_id=1, source_target_pairs={{0,8},{8,16},{16,24},{24,32},{32,40},{40,48},{48,56},{56,64},{64,7... | collective-permute-start | bytes 1572872 | tf_op jit(solution)/shard_map/while/body/eval_jaxpr/ppermute | solution.py:21
  330.6 9.2 %collective-permute-start = (bf16[2,512,256]{1,2,0:T(8,128)(2,1)}, bf16[2,512,256]{1,2,0:T(8,128)(2,1)S(1)}, u32[]{:S(2)}, u32[]{:S(2)}) collective-permute-start(bf16[2,512,256]{1,2,0:T(8,128)(2,1)} %get-tuple-element.572), channel_id=1, source_target_pairs={{0,8},{8,16},{16,24},{24,32},{32,40},{40,48},{48,56},{56,64},{64,7... | collective-permute-start | bytes 1572872 | tf_op jit(solution)/shard_map/while/body/eval_jaxpr/ppermute | solution.py:21
  345.8 9.2 %collective-permute-start = (bf16[2,512,256]{1,2,0:T(8,128)(2,1)}, bf16[2,512,256]{1,2,0:T(8,128)(2,1)S(1)}, u32[]{:S(2)}, u32[]{:S(2)}) collective-permute-start(bf16[2,512,256]{1,2,0:T(8,128)(2,1)} %get-tuple-element.572), channel_id=1, source_target_pairs={{0,8},{8,16},{16,24},{24,32},{32,40},{40,48},{48,56},{56,64},{64,7... | collective-permute-start | bytes 1572872 | tf_op jit(solution)/shard_map/while/body/eval_jaxpr/ppermute | solution.py:21
  361.1 9.2 %collective-permute-start = (bf16[2,512,256]{1,2,0:T(8,128)(2,1)}, bf16[2,512,256]{1,2,0:T(8,128)(2,1)S(1)}, u32[]{:S(2)}, u32[]{:S(2)}) collective-permute-start(bf16[2,512,256]{1,2,0:T(8,128)(2,1)} %get-tuple-element.572), channel_id=1, source_target_pairs={{0,8},{8,16},{16,24},{24,32},{32,40},{40,48},{48,56},{56,64},{64,7... | collective-permute-start | bytes 1572872 | tf_op jit(solution)/shard_map/while/body/eval_jaxpr/ppermute | solution.py:21
  376.3 9.2 %collective-permute-start = (bf16[2,512,256]{1,2,0:T(8,128)(2,1)}, bf16[2,512,256]{1,2,0:T(8,128)(2,1)S(1)}, u32[]{:S(2)}, u32[]{:S(2)}) collective-permute-start(bf16[2,512,256]{1,2,0:T(8,128)(2,1)} %get-tuple-element.572), channel_id=1, source_target_pairs={{0,8},{8,16},{16,24},{24,32},{32,40},{40,48},{48,56},{56,64},{64,7... | collective-permute-start | bytes 1572872 | tf_op jit(solution)/shard_map/while/body/eval_jaxpr/ppermute | solution.py:21
  391.6 9.2 %collective-permute-start = (bf16[2,512,256]{1,2,0:T(8,128)(2,1)}, bf16[2,512,256]{1,2,0:T(8,128)(2,1)S(1)}, u32[]{:S(2)}, u32[]{:S(2)}) collective-permute-start(bf16[2,512,256]{1,2,0:T(8,128)(2,1)} %get-tuple-element.572), channel_id=1, source_target_pairs={{0,8},{8,16},{16,24},{24,32},{32,40},{40,48},{48,56},{56,64},{64,7... | collective-permute-start | bytes 1572872 | tf_op jit(solution)/shard_map/while/body/eval_jaxpr/ppermute | solution.py:21
  406.8 9.2 %collective-permute-start = (bf16[2,512,256]{1,2,0:T(8,128)(2,1)}, bf16[2,512,256]{1,2,0:T(8,128)(2,1)S(1)}, u32[]{:S(2)}, u32[]{:S(2)}) collective-permute-start(bf16[2,512,256]{1,2,0:T(8,128)(2,1)} %get-tuple-element.572), channel_id=1, source_target_pairs={{0,8},{8,16},{16,24},{24,32},{32,40},{40,48},{48,56},{56,64},{64,7... | collective-permute-start | bytes 1572872 | tf_op jit(solution)/shard_map/while/body/eval_jaxpr/ppermute | solution.py:21
  423.4 5.5 fusion.33
  428.9 7.3 %add_convert_fusion = bf16[512,4096]{1,0:T(8,128)(2,1)} fusion(f32[512,4096]{1,0:T(8,128)} %fusion.33, bf16[512,256]{0,1:T(8,128)(2,1)S(1)} %bitcast.61, bf16[256,4096]{1,0:T(8,128)(2,1)} %all-gather.11.cloned.1.call-done), kind=kOutput, calls=%fused_computation.50 | convolution fusion | flops 1080033280 | bytes 14942208 | tf_op jit(solution)/shard_map/dot_general | solution.py:175
  436.8 167.8 %reduce-scatter.2.cloned.1.call-done = bf16[512,512]{1,0:T(8,128)(2,1)} async-done(((bf16[512,4096]{1,0:T(8,128)(2,1)}), bf16[512,512]{1,0:T(8,128)(2,1)}) %reduce-scatter.2.cloned.1.call-update) | async-done | bytes 524304 | tf_op jit(solution)/shard_map/reduce_scatter | solution.py:183
  (274 shorter events, 92.4 us)
Async XLA Ops:
  7.2 416.2 %copy-start = (bf16[64,4096]{1,0:T(8,128)(2,1)S(1)}, bf16[64,4096]{1,0:T(8,128)(2,1)}, u32[]{:S(2)}) copy-start(bf16[64,4096]{1,0:T(8,128)(2,1)} %param.31) | copy-start | bytes 1572868
  7.2 63.9 %all-gather.5.cloned.1.call-start = ((), (), s32[]{:S(2)}) async-start(), calls=%async_computation.1 | async-start | bytes 2162688 | tf_op jit(solution)/shard_map/all_gather | solution.py:113
  7.9 124.1 %all-gather.9.cloned.1.call-start = ((), (), s32[]{:S(2)}) async-start(), calls=%async_computation.3 | async-start | bytes 2162688 | tf_op jit(solution)/shard_map/all_gather | solution.py:112
  8.7 184.3 %all-gather.7.cloned.1.call-start = ((), (), s32[]{:S(2)}) async-start(), calls=%async_computation.2 | async-start | bytes 2162688 | tf_op jit(solution)/shard_map/all_gather | solution.py:114
  9.4 419.5 %all-gather.11.cloned.1.call-start = ((), (), s32[]{:S(2)}) async-start(), calls=%async_computation.4 | async-start | bytes 2162688 | tf_op jit(solution)/shard_map/all_gather | solution.py:177
  10.0 594.7 %reduce-scatter.2.cloned.1.call-start = ((), (), s32[]{:S(2)}) async-start(), calls=%async_computation.5 | async-start | bytes 4718592 | tf_op jit(solution)/shard_map/reduce_scatter | solution.py:183
  10.0 3.1 copy-start.8
  10.1 4.3 copy-start.7
  20.1 55.1 %copy-start.1 = (bf16[4096,64]{0,1:T(8,128)(2,1)S(1)}, bf16[4096,64]{0,1:T(8,128)(2,1)}, u32[]{:S(2)}) copy-start(bf16[4096,64]{0,1:T(8,128)(2,1)} %param.26) | copy-start | bytes 1572868
  79.0 57.2 %copy-start.2 = (bf16[4096,64]{0,1:T(8,128)(2,1)S(1)}, bf16[4096,64]{0,1:T(8,128)(2,1)}, u32[]{:S(2)}) copy-start(bf16[4096,64]{0,1:T(8,128)(2,1)} %param.24) | copy-start | bytes 1572868
  202.7 2.2 copy-start.6
  204.9 10.5 %collective-permute-start = (bf16[2,512,256]{1,2,0:T(8,128)(2,1)}, bf16[2,512,256]{1,2,0:T(8,128)(2,1)S(1)}, u32[]{:S(2)}, u32[]{:S(2)}) collective-permute-start(bf16[2,512,256]{1,2,0:T(8,128)(2,1)} %get-tuple-element.572), channel_id=1, source_target_pairs={{0,8},{8,16},{16,24},{24,32},{32,40},{40,48},{48,56},{56,64},{64,7... | collective-permute-start | bytes 1572872 | tf_op jit(solution)/shard_map/while/body/eval_jaxpr/ppermute | solution.py:21
  219.7 9.6 %collective-permute-start = (bf16[2,512,256]{1,2,0:T(8,128)(2,1)}, bf16[2,512,256]{1,2,0:T(8,128)(2,1)S(1)}, u32[]{:S(2)}, u32[]{:S(2)}) collective-permute-start(bf16[2,512,256]{1,2,0:T(8,128)(2,1)} %get-tuple-element.572), channel_id=1, source_target_pairs={{0,8},{8,16},{16,24},{24,32},{32,40},{40,48},{48,56},{56,64},{64,7... | collective-permute-start | bytes 1572872 | tf_op jit(solution)/shard_map/while/body/eval_jaxpr/ppermute | solution.py:21
  229.3 1.8 copy-start.3
  233.6 10.6 %collective-permute-start = (bf16[2,512,256]{1,2,0:T(8,128)(2,1)}, bf16[2,512,256]{1,2,0:T(8,128)(2,1)S(1)}, u32[]{:S(2)}, u32[]{:S(2)}) collective-permute-start(bf16[2,512,256]{1,2,0:T(8,128)(2,1)} %get-tuple-element.572), channel_id=1, source_target_pairs={{0,8},{8,16},{16,24},{24,32},{32,40},{40,48},{48,56},{56,64},{64,7... | collective-permute-start | bytes 1572872 | tf_op jit(solution)/shard_map/while/body/eval_jaxpr/ppermute | solution.py:21
  248.5 9.5 %collective-permute-start = (bf16[2,512,256]{1,2,0:T(8,128)(2,1)}, bf16[2,512,256]{1,2,0:T(8,128)(2,1)S(1)}, u32[]{:S(2)}, u32[]{:S(2)}) collective-permute-start(bf16[2,512,256]{1,2,0:T(8,128)(2,1)} %get-tuple-element.572), channel_id=1, source_target_pairs={{0,8},{8,16},{16,24},{24,32},{32,40},{40,48},{48,56},{56,64},{64,7... | collective-permute-start | bytes 1572872 | tf_op jit(solution)/shard_map/while/body/eval_jaxpr/ppermute | solution.py:21
  262.4 8.8 %collective-permute-start = (bf16[2,512,256]{1,2,0:T(8,128)(2,1)}, bf16[2,512,256]{1,2,0:T(8,128)(2,1)S(1)}, u32[]{:S(2)}, u32[]{:S(2)}) collective-permute-start(bf16[2,512,256]{1,2,0:T(8,128)(2,1)} %get-tuple-element.572), channel_id=1, source_target_pairs={{0,8},{8,16},{16,24},{24,32},{32,40},{40,48},{48,56},{56,64},{64,7... | collective-permute-start | bytes 1572872 | tf_op jit(solution)/shard_map/while/body/eval_jaxpr/ppermute | solution.py:21
  271.2 1.8 copy-start.3
  275.5 8.8 %collective-permute-start = (bf16[2,512,256]{1,2,0:T(8,128)(2,1)}, bf16[2,512,256]{1,2,0:T(8,128)(2,1)S(1)}, u32[]{:S(2)}, u32[]{:S(2)}) collective-permute-start(bf16[2,512,256]{1,2,0:T(8,128)(2,1)} %get-tuple-element.572), channel_id=1, source_target_pairs={{0,8},{8,16},{16,24},{24,32},{32,40},{40,48},{48,56},{56,64},{64,7... | collective-permute-start | bytes 1572872 | tf_op jit(solution)/shard_map/while/body/eval_jaxpr/ppermute | solution.py:21
  288.7 8.8 %collective-permute-start = (bf16[2,512,256]{1,2,0:T(8,128)(2,1)}, bf16[2,512,256]{1,2,0:T(8,128)(2,1)S(1)}, u32[]{:S(2)}, u32[]{:S(2)}) collective-permute-start(bf16[2,512,256]{1,2,0:T(8,128)(2,1)} %get-tuple-element.572), channel_id=1, source_target_pairs={{0,8},{8,16},{16,24},{24,32},{32,40},{40,48},{48,56},{56,64},{64,7... | collective-permute-start | bytes 1572872 | tf_op jit(solution)/shard_map/while/body/eval_jaxpr/ppermute | solution.py:21
  301.8 9.2 %collective-permute-start = (bf16[2,512,256]{1,2,0:T(8,128)(2,1)}, bf16[2,512,256]{1,2,0:T(8,128)(2,1)S(1)}, u32[]{:S(2)}, u32[]{:S(2)}) collective-permute-start(bf16[2,512,256]{1,2,0:T(8,128)(2,1)} %get-tuple-element.572), channel_id=1, source_target_pairs={{0,8},{8,16},{16,24},{24,32},{32,40},{40,48},{48,56},{56,64},{64,7... | collective-permute-start | bytes 1572872 | tf_op jit(solution)/shard_map/while/body/eval_jaxpr/ppermute | solution.py:21
  311.0 1.8 copy-start.3
  315.3 10.9 %collective-permute-start = (bf16[2,512,256]{1,2,0:T(8,128)(2,1)}, bf16[2,512,256]{1,2,0:T(8,128)(2,1)S(1)}, u32[]{:S(2)}, u32[]{:S(2)}) collective-permute-start(bf16[2,512,256]{1,2,0:T(8,128)(2,1)} %get-tuple-element.572), channel_id=1, source_target_pairs={{0,8},{8,16},{16,24},{24,32},{32,40},{40,48},{48,56},{56,64},{64,7... | collective-permute-start | bytes 1572872 | tf_op jit(solution)/shard_map/while/body/eval_jaxpr/ppermute | solution.py:21
  326.3 1.8 copy-start.3
  330.6 10.9 %collective-permute-start = (bf16[2,512,256]{1,2,0:T(8,128)(2,1)}, bf16[2,512,256]{1,2,0:T(8,128)(2,1)S(1)}, u32[]{:S(2)}, u32[]{:S(2)}) collective-permute-start(bf16[2,512,256]{1,2,0:T(8,128)(2,1)} %get-tuple-element.572), channel_id=1, source_target_pairs={{0,8},{8,16},{16,24},{24,32},{32,40},{40,48},{48,56},{56,64},{64,7... | collective-permute-start | bytes 1572872 | tf_op jit(solution)/shard_map/while/body/eval_jaxpr/ppermute | solution.py:21
  345.8 10.9 %collective-permute-start = (bf16[2,512,256]{1,2,0:T(8,128)(2,1)}, bf16[2,512,256]{1,2,0:T(8,128)(2,1)S(1)}, u32[]{:S(2)}, u32[]{:S(2)}) collective-permute-start(bf16[2,512,256]{1,2,0:T(8,128)(2,1)} %get-tuple-element.572), channel_id=1, source_target_pairs={{0,8},{8,16},{16,24},{24,32},{32,40},{40,48},{48,56},{56,64},{64,7... | collective-permute-start | bytes 1572872 | tf_op jit(solution)/shard_map/while/body/eval_jaxpr/ppermute | solution.py:21
  361.1 10.9 %collective-permute-start = (bf16[2,512,256]{1,2,0:T(8,128)(2,1)}, bf16[2,512,256]{1,2,0:T(8,128)(2,1)S(1)}, u32[]{:S(2)}, u32[]{:S(2)}) collective-permute-start(bf16[2,512,256]{1,2,0:T(8,128)(2,1)} %get-tuple-element.572), channel_id=1, source_target_pairs={{0,8},{8,16},{16,24},{24,32},{32,40},{40,48},{48,56},{56,64},{64,7... | collective-permute-start | bytes 1572872 | tf_op jit(solution)/shard_map/while/body/eval_jaxpr/ppermute | solution.py:21
  372.0 1.8 copy-start.3
  376.3 10.9 %collective-permute-start = (bf16[2,512,256]{1,2,0:T(8,128)(2,1)}, bf16[2,512,256]{1,2,0:T(8,128)(2,1)S(1)}, u32[]{:S(2)}, u32[]{:S(2)}) collective-permute-start(bf16[2,512,256]{1,2,0:T(8,128)(2,1)} %get-tuple-element.572), channel_id=1, source_target_pairs={{0,8},{8,16},{16,24},{24,32},{32,40},{40,48},{48,56},{56,64},{64,7... | collective-permute-start | bytes 1572872 | tf_op jit(solution)/shard_map/while/body/eval_jaxpr/ppermute | solution.py:21
  391.6 10.9 %collective-permute-start = (bf16[2,512,256]{1,2,0:T(8,128)(2,1)}, bf16[2,512,256]{1,2,0:T(8,128)(2,1)S(1)}, u32[]{:S(2)}, u32[]{:S(2)}) collective-permute-start(bf16[2,512,256]{1,2,0:T(8,128)(2,1)} %get-tuple-element.572), channel_id=1, source_target_pairs={{0,8},{8,16},{16,24},{24,32},{32,40},{40,48},{48,56},{56,64},{64,7... | collective-permute-start | bytes 1572872 | tf_op jit(solution)/shard_map/while/body/eval_jaxpr/ppermute | solution.py:21
  406.8 10.9 %collective-permute-start = (bf16[2,512,256]{1,2,0:T(8,128)(2,1)}, bf16[2,512,256]{1,2,0:T(8,128)(2,1)S(1)}, u32[]{:S(2)}, u32[]{:S(2)}) collective-permute-start(bf16[2,512,256]{1,2,0:T(8,128)(2,1)} %get-tuple-element.572), channel_id=1, source_target_pairs={{0,8},{8,16},{16,24},{24,32},{32,40},{40,48},{48,56},{56,64},{64,7... | collective-permute-start | bytes 1572872 | tf_op jit(solution)/shard_map/while/body/eval_jaxpr/ppermute | solution.py:21
  417.8 1.8 copy-start.3
  (25 other events, 31.9 us)
Sparse Core Ops, SparseCore 0:
  9.9 61.1 all-gather.4
  72.9 59.0 all-gather.8
  133.8 59.0 all-gather.6
  194.6 64.1 all-gather.10
  436.4 168.2 reduce-scatter.1
where the time goes:
time: 613 us; the launch traced here: 611 us
  waiting for transfers between devices  393 us (64%)
  starting transfers between devices  81.7 us (13%)
  matrix products  76.6 us (12%)
  other arithmetic  27.2 us (4%)
  local copies, waits for them, and re-layouts  17.7 us (3%)
  between operations  14.1 us (2%)
    reduce_scatter x1, waiting for transfers between devices, body(): lax.psum_scatter(summand_terms.astype(jnp.bfloat16), 'head', scatter_dime...  168 us
    ppermute x15, starting transfers between devices, from_behind(): return lax.ppermute(value, axis, pairs)  81.5 us
    ppermute x15, waiting for transfers between devices, from_behind(): return lax.ppermute(value, axis, pairs)  68.9 us
    all_gather x1, waiting for transfers between devices, body(): lax.all_gather(query_weight, 'seq', axis=0, tiled=True)  53 us
    all_gather x1, waiting for transfers between devices, body(): lax.all_gather(key_weight, 'seq', axis=0, tiled=True)  50.9 us
    all_gather x1, waiting for transfers between devices, body(): lax.all_gather(value_weight, 'seq', axis=0, tiled=True)  49.6 us
    dot_general x16, matrix products, one_block(): jnp.einsum('hqk,khd->hqd', weights.astype(jnp.bfloat16), value_tile, pref...  24.8 us
    while x90, local copies, waits for them, and re-layouts  14.9 us
  transfers between devices with their start and end apart: 20, of which 19 were waited for; matrix products, arithmetic and copies ran while one was open for 18% of the time, Pallas kernels for 0%

commit v1 on v0

v1 whole, which is shorter than its diff:
```python
import math

import jax
import jax.numpy as jnp
import numpy as np
from jax import lax
from jax.experimental import pallas as pl
from jax.experimental.pallas import tpu as pltpu
from jax.sharding import PartitionSpec as P

EPS = 1e-05
ADAPTER_SCALING = 0.5
ROPE_BASE = 10000.0
MASKED = -1e30
D = 4096
HD = 128
TOK = 512
CHIP = 2 * TOK
MESH = pl.DeviceIdType.MESH
F32 = jnp.float32
BF16 = jnp.bfloat16
VMEM_BYTES = 56 * 1024 * 1024


def spot():
    seq = lax.axis_index("seq")
    head = lax.axis_index("head")
    return seq // 8, (seq // 2) % 4, seq % 2, head // 2, head % 2


def seq_of(z, x, core):
    return z * 8 + x * 2 + core


def greet(partners):
    barrier = pltpu.get_barrier_semaphore()
    for partner in partners:
        pl.semaphore_signal(barrier, inc=1, device_id=partner, device_id_type=MESH)
    pl.semaphore_wait(barrier, len(partners))


def remote(source, target, send, receive, device):
    return pltpu.make_async_remote_copy(
        src_ref=source,
        dst_ref=target,
        send_sem=send,
        recv_sem=receive,
        device_id=device,
        device_id_type=MESH,
    )


def dot(a, b):
    return jnp.dot(a, b, preferred_element_type=F32)


def dot_nt(a, b):
    return lax.dot_general(a, b, (((1,), (1,)), ((), ())), preferred_element_type=F32)


def times(value, n):
    return jnp.concatenate([value] * n, axis=1)


class Ring:
    def __init__(self, view, receive, send, place, right, left):
        self.view, self.receive, self.send = view, receive, send
        self.place, self.right, self.left = place, right, left
        self.open = []

    def slot(self, d, step):
        return d * 4 + (self.place + step) % 4

    def start(self, source, target, receive, device):
        copy = remote(source, target, self.send.at[len(self.open)], receive, device)
        copy.start()
        self.open.append(copy)

    def push(self, d, step, device):
        slot = self.slot(d, step)
        self.start(self.view(slot), self.view(slot), self.receive.at[slot], device)

    def push_own(self, d):
        self.push(d, 0, self.right)
        self.push(d, 0, self.left)

    def arrived(self, d, step):
        slot = self.slot(d, step)
        ref = self.view(slot)
        remote(ref, ref, self.send.at[0], self.receive.at[slot], self.right).wait_recv()

    def own(self, d):
        self.arrived(d, 0)
        self.push_own(d)

    def from_left(self, d):
        self.arrived(d, 3)
        if d % 2 == 0:
            self.push(d, 3, self.right)

    def from_right(self, d):
        self.arrived(d, 1)
        if d % 2 == 1:
            self.push(d, 1, self.left)

    def across(self, d):
        self.arrived(d, 2)

    def finish(self):
        for copy in self.open:
            copy.wait_send()


def project_kernel(
    act, gain, wq, wk, wv, down_q, down_k, down_v, up_q, up_k, up_v, tables, bases,
    q_out, k_out, v_out,
    raw, normed, stage, weights, downs, down_all, up_all, total,
    load, receive, send, norm_receive, norm_send,
):
    z, x, core, y, zh = spot()
    head = lax.axis_index("head")
    sibling = (seq_of(z, x, 1 - core), head)
    right = (seq_of(z, (x + 1) % 4, core), head)
    left = (seq_of(z, (x + 3) % 4, core), head)

    loads = []
    for part in range(4):
        rows = pl.ds(part * 128, 128)
        loads.append(pltpu.make_async_copy(act.at[rows], raw.at[rows], load.at[part]))
    for index, ref in enumerate((down_q, down_k, down_v)):
        loads.append(pltpu.make_async_copy(ref, downs.at[index], load.at[4 + index]))
    up_all[...] = jnp.zeros_like(up_all)
    columns = pl.ds(pl.multiple_of(head * 256 + core * 128, 128), 128)
    for index, ref in enumerate((up_q, up_k, up_v)):
        target = up_all.at[pl.ds(index * 64, 64), pl.ds(index * 128, 128)]
        loads.append(pltpu.make_async_copy(ref.at[:, columns], target, load.at[7 + index]))
    for copy in loads:
        copy.start()
    for side in range(2):
        for index, ref in enumerate((wq, wk, wv)):
            stage[side, :, index * 128 : index * 128 + 128] = ref[:, side * 128 : side * 128 + 128]

    planes = [(z + e) % 4 for e in range(1, 4)]
    greet(
        [sibling, right, left]
        + [(seq_of(plane, x, side), head) for plane in planes for side in range(2)]
    )

    ring = Ring(lambda slot: weights.at[slot], receive, send, x, right, left)
    half = pl.ds(pl.multiple_of(core * 128, 128), 128)
    other = pl.ds(pl.multiple_of(128 - core * 128, 128), 128)
    ring.start(stage.at[1 - core], weights.at[x, half], receive.at[x], sibling)
    for e, plane in zip(range(1, 4), planes):
        for side in range(2):
            slot = e * 4 + x
            ring.start(
                stage.at[side],
                weights.at[slot, half],
                receive.at[slot],
                (seq_of(plane, x, side), head),
            )
    weights[x, half, :] = stage[core]

    norm_copies = []

    def normalize(part):
        loads[part].wait()

        def tile(index, carry):
            row = part * 128 + index * 16
            wide = raw[pl.ds(row, 16), :].astype(F32)
            mean_square = jnp.mean(wide * wide, axis=-1, keepdims=True)
            result = (wide * lax.rsqrt(mean_square + EPS) * gain[...]).astype(BF16)
            place = pl.ds(pl.multiple_of(core * TOK + row, 16), 16)
            for chunk in range(16):
                normed[chunk, place, :] = result[:, chunk * 256 : chunk * 256 + 256]
            return carry

        lax.fori_loop(0, 8, tile, 0)
        rows = pl.ds(pl.multiple_of(core * TOK + part * 128, 128), 128)
        copy = remote(
            normed.at[:, rows],
            normed.at[:, rows],
            norm_send.at[part],
            norm_receive.at[part],
            sibling,
        )
        copy.start()
        norm_copies.append(copy)

    def reduced(side):
        for block in range(2):
            rows = pl.ds(pl.multiple_of(side * TOK + block * 256, 256), 256)

            def step(chunk, carry):
                return carry + dot(normed[chunk, rows, :], down_all[chunk])

            low = lax.fori_loop(0, 16, step, jnp.zeros((256, 192), F32)).astype(BF16)
            total[rows, :] = ADAPTER_SCALING * dot(low, up_all[...])

    def accumulate(d):
        def block(index, carry):
            rows = pl.ds(pl.multiple_of(index * 256, 256), 256)
            value = total[rows, :]
            for step in range(4):
                slot = ring.slot(d, step)
                chunk = ((z + 4 - d) % 4) * 4 + (x + step) % 4
                value = value + dot(normed[chunk, rows, :], weights[slot])
            total[rows, :] = value
            return carry

        lax.fori_loop(0, 4, block, 0)

    normalize(0)
    piece = weights.at[x, other]
    remote(piece, piece, send.at[0], receive.at[x], sibling).wait_recv()
    ring.push_own(0)
    normalize(1)
    normalize(2)
    ring.own(1)
    normalize(3)
    ring.from_left(0)
    ring.from_right(0)
    for copy in loads[4:]:
        copy.wait()

    def join(chunk, carry):
        rows = pl.ds(pl.multiple_of(chunk * 256, 256), 256)
        down_all[chunk] = jnp.concatenate([downs[index, rows, :] for index in range(3)], axis=1)
        return carry

    lax.fori_loop(0, 16, join, 0)
    reduced(core)
    ring.own(2)
    for part in range(4):
        rows = pl.ds(pl.multiple_of((1 - core) * TOK + part * 128, 128), 128)
        ref = normed.at[:, rows]
        remote(ref, ref, norm_send.at[part], norm_receive.at[part], sibling).wait_recv()
    reduced(1 - core)
    ring.from_left(1)
    ring.from_right(1)
    ring.own(3)
    ring.across(0)
    accumulate(0)
    ring.from_left(2)
    ring.from_right(2)
    ring.across(1)
    accumulate(1)
    ring.from_left(3)
    ring.from_right(3)
    ring.across(2)
    accumulate(2)
    ring.across(3)
    accumulate(3)

    base = bases[pl.ds(z * 4 + x, 1)]
    base_cos, base_sin = base[0, 0:1, :], base[0, 1:2, :]

    def turn(index, carry):
        rows = pl.ds(pl.multiple_of(index * 128, 128), 128)
        cos_row, sin_row = tables[0, rows, :], tables[1, rows, :]
        cos = cos_row * base_cos - sin_row * base_sin
        sin = sin_row * base_cos + cos_row * base_sin
        for number, ref in enumerate((q_out, k_out)):
            value = total[rows, number * 128 : number * 128 + 128]
            value = value * cos + pltpu.roll(value, 64, 1) * sin
            if number == 0:
                value = value * (math.log2(math.e) / math.sqrt(HD))
            ref[rows, :] = value.astype(BF16)
        v_out[rows, :] = total[rows, 256:384].astype(BF16)
        return carry

    lax.fori_loop(0, 8, turn, 0)
    ring.finish()
    for copy in norm_copies:
        copy.wait_send()


def attend_kernel(
    shifted, q, k, v, mixed, log_sums, kv, top, total, load, receive, send
):
    z, x, core, y, zh = spot()
    head = lax.axis_index("head")
    right = (seq_of(z, (x + 1) % 4, core), head)
    left = (seq_of(z, (x + 3) % 4, core), head)
    after = (seq_of((z + 1) % 4, x, core), head)
    before = (seq_of((z + 3) % 4, x, core), head)

    loads = []
    for part in range(2):
        rows = pl.ds(part * TOK, TOK)
        slot = part * 4 + x
        for index, ref in enumerate((k, v)):
            target = kv.at[slot, :, pl.ds(index * 128, 128)]
            loads.append(pltpu.make_async_copy(ref.at[rows], target, load.at[part * 2 + index]))
    for copy in loads:
        copy.start()

    def ones(slot, carry):
        kv[slot, :, 256:384] = jnp.ones((TOK, 128), BF16)
        return carry

    lax.fori_loop(0, 16, ones, 0)
    greet([right, left, after, before])
    for copy in loads:
        copy.wait()

    ring = Ring(lambda slot: kv.at[slot, :, pl.ds(0, 256)], receive, send, x, right, left)
    for part in range(2):
        source, slot = ring.view(ring.slot(part, 0)), ring.slot(part + 2, 0)
        ring.push_own(part)
        ring.start(source, ring.view(slot), receive.at[slot], after)

    for index in range(4):
        rows = pl.ds(index * 256, 256)
        keys = index * 256 + 256
        pieces = []
        for part in range((keys + TOK - 1) // TOK):
            count = min(keys - part * TOK, TOK)
            slot = ring.slot(part, 0)
            scores = dot_nt(q[rows, :], kv[slot, 0:count, 0:128])
            row = index * 256 + lax.broadcasted_iota(jnp.int32, scores.shape, 0)
            column = part * TOK + lax.broadcasted_iota(jnp.int32, scores.shape, 1)
            pieces.append((slot, count, jnp.where(column <= row, scores, MASKED)))
        highest = jnp.max(pieces[0][2], axis=1, keepdims=True)
        for slot, count, scores in pieces[1:]:
            highest = jnp.maximum(highest, jnp.max(scores, axis=1, keepdims=True))
        highest = jnp.broadcast_to(highest, (256, 128))
        value = jnp.zeros((256, 256), F32)
        for slot, count, scores in pieces:
            soft = jnp.exp2(scores - times(highest, count // 128)).astype(BF16)
            value = value + dot(soft, kv[slot, 0:count, 128:384])
        top[rows, :] = highest
        total[rows, :] = value

    def attend(d, step, bias):
        first, second = ring.slot(d, step), ring.slot(d + 1, step)

        def block(index, carry):
            rows = pl.ds(pl.multiple_of(index * 256, 256), 256)
            query = q[rows, :]
            one = dot_nt(query, kv[first, :, 0:128])
            two = dot_nt(query, kv[second, :, 0:128])
            highest = jnp.max(jnp.maximum(one, two), axis=1, keepdims=True)
            old = top[rows, :]
            new = jnp.maximum(old, highest + bias)
            level = times(new - bias, 4)
            value = total[rows, :] * times(jnp.exp2(old - new), 2)
            value = value + dot(jnp.exp2(one - level).astype(BF16), kv[first, :, 128:384])
            value = value + dot(jnp.exp2(two - level).astype(BF16), kv[second, :, 128:384])
            top[rows, :] = new
            total[rows, :] = value
            return carry

        lax.fori_loop(0, 4, block, 0)

    def attend_own_plane(step):
        @pl.when((x + step) % 4 < x)
        def _():
            attend(0, step, 0.0)

    flag = shifted[head * 2 + core]
    reaches = (z % 2) * (1 - flag) + (1 - z % 2) * flag
    bias = (reaches.astype(F32) - 1.0) * (-MASKED)

    ring.from_left(0)
    ring.from_right(1)
    ring.from_left(1)
    ring.from_right(0)
    ring.own(2)
    ring.own(3)
    attend_own_plane(3)
    attend_own_plane(1)
    attend(2, 0, bias)
    ring.across(0)
    ring.across(1)
    ring.from_left(2)
    ring.from_right(3)
    attend_own_plane(2)
    ring.from_left(3)
    attend(2, 3, bias)
    ring.from_right(2)
    attend(2, 1, bias)
    ring.across(2)
    ring.across(3)
    attend(2, 2, bias)

    def close(index, carry):
        rows = pl.ds(pl.multiple_of(index * 256, 256), 256)
        weight = total[rows, 128:256]
        mixed[rows, :] = (total[rows, 0:128] / weight).astype(BF16)
        log_sums[rows, :] = (top[rows, :] + jnp.log2(weight)) * math.log(2.0)
        return carry

    lax.fori_loop(0, 4, close, 0)
    ring.finish()


def output_kernel(
    mixed, log_sums, weight, down, up, out, sums_out, held, sums, up_here, low, total,
    load, receive, send, sums_receive,
):
    z, x, core, y, zh = spot()
    seq = lax.axis_index("seq")
    head = lax.axis_index("head")
    sibling = (seq_of(z, x, 1 - core), head)
    right = (seq, ((y + 1) % 4) * 2 + zh)
    left = (seq, ((y + 3) % 4) * 2 + zh)
    partners = [(seq_of(z, x, side), y * 2 + 1 - zh) for side in range(2)]
    greet([sibling, right, left] + partners)

    ring = Ring(lambda slot: held.at[slot], receive, send, y, right, left)
    columns = pl.ds(pl.multiple_of(core * 128, 128), 128)
    others = pl.ds(pl.multiple_of(128 - core * 128, 128), 128)
    loads = []
    for part in range(2):
        slot = ring.slot(2 + part, 0)
        for side in range(2):
            source = mixed.at[pl.ds(side * TOK + part * 256, 256)]
            ring.start(source, held.at[slot, :, columns], receive.at[slot], partners[side])
    for part in range(2):
        slot = ring.slot(part, 0)
        source = mixed.at[pl.ds(pl.multiple_of((1 - core) * TOK + part * 256, 256), 256)]
        ring.start(source, held.at[slot, :, columns], receive.at[slot], sibling)
        source = mixed.at[pl.ds(pl.multiple_of(core * TOK + part * 256, 256), 256)]
        loads.append(pltpu.make_async_copy(source, held.at[slot, :, columns], load.at[part]))
    source = log_sums.at[pl.ds(pl.multiple_of((1 - core) * TOK, TOK), TOK)]
    ring.start(source, sums.at[core], sums_receive, sibling)
    source = log_sums.at[pl.ds(pl.multiple_of(core * TOK, TOK), TOK)]
    loads.append(pltpu.make_async_copy(source, sums.at[core], load.at[2]))
    source = up.at[:, pl.ds(pl.multiple_of(head * 512, 512), 512)]
    loads.append(pltpu.make_async_copy(source, up_here, load.at[3]))
    for copy in loads:
        copy.start()
    total[...] = jnp.zeros_like(total)
    low[...] = jnp.zeros_like(low)
    for copy in loads:
        copy.wait()
    for part in range(2):
        slot = ring.slot(part, 0)
        piece = held.at[slot, :, others]
        remote(piece, piece, send.at[0], receive.at[slot], sibling).wait_recv()
        ring.push_own(part)

    def add(d, step):
        rows = pl.ds((d % 2) * 256, 256)
        group = ((y + step) % 4) * 2 + (zh + d // 2) % 2
        block = held[ring.slot(d, step)]
        matrix = jnp.concatenate([weight[group * 4 + j] for j in range(4)], axis=1)
        total[rows, :] += dot(block, matrix)
        low[rows, :] += dot(block, down[group])

    ring.own(2)
    ring.own(3)
    add(0, 0)
    add(1, 0)
    for d in range(2):
        ring.from_left(d)
        ring.from_right(d)
        add(d, 3)
        add(d, 1)
    add(2, 0)
    add(3, 0)
    for d in range(2):
        ring.across(d)
        add(d, 2)
    for d in range(2, 4):
        ring.from_left(d)
        ring.from_right(d)
        add(d, 3)
        add(d, 1)
    for d in range(2, 4):
        ring.across(d)
        add(d, 2)

    remote(sums.at[1 - core], sums.at[1 - core], send.at[0], sums_receive, sibling).wait_recv()
    lane = lax.broadcasted_iota(jnp.int32, (TOK, 128), 1)
    sums_out[...] = jnp.where(lane == 0, sums[0], sums[1])[:, 0:2]
    out[...] = (
        total[...] + ADAPTER_SCALING * dot(low[...].astype(BF16), up_here[...])
    ).astype(BF16)
    ring.finish()


def rope_tables():
    frequency = ROPE_BASE ** (-2.0 * np.arange(64, dtype=np.float64) / HD)
    sign = np.concatenate([-np.ones(64), np.ones(64)])

    def table(positions):
        angles = positions[:, None] * np.concatenate([frequency, frequency])[None, :]
        return np.cos(angles), np.sin(angles) * sign

    tables = np.stack(table(np.arange(CHIP, dtype=np.float64)))
    bases = np.stack(table(np.arange(16, dtype=np.float64) * CHIP), axis=1)
    return tables.astype(np.float32), bases.astype(np.float32)


VMEM = pl.BlockSpec(memory_space=pltpu.VMEM)
ANY = pl.BlockSpec(memory_space=pl.ANY)
SMEM = pl.BlockSpec(memory_space=pltpu.SMEM)
DMA = pltpu.SemaphoreType.DMA


def call(kernel, outs, in_specs, scratch, number):
    return pl.pallas_call(
        kernel,
        out_shape=tuple(jax.ShapeDtypeStruct(shape, kind) for shape, kind in outs),
        in_specs=in_specs,
        out_specs=tuple(VMEM for _ in outs),
        scratch_shapes=scratch,
        compiler_params=pltpu.CompilerParams(
            collective_id=number, has_side_effects=True, vmem_limit_bytes=VMEM_BYTES
        ),
    )


def body(
    activations,
    norm_gain,
    shifted,
    query_weight,
    key_weight,
    value_weight,
    output_weight,
    query_down,
    query_up,
    key_down,
    key_up,
    value_down,
    value_up,
    output_down,
    output_up_matrix,
):
    pairs = []
    for h in range(8):
        for j in range(4):
            for g in range(8):
                pairs.append(((h * 4 + j) * 8 + g, (g * 4 + j) * 8 + h))
    turned = lax.ppermute(output_weight, ("seq", "head"), pairs)
    columns = lax.all_gather(turned, "seq", axis=0)

    tables, bases = rope_tables()
    half = ((CHIP, HD), BF16)
    q, k, v = call(
        project_kernel,
        [half, half, half],
        [ANY] + [VMEM] * 4 + [ANY] * 6 + [VMEM] * 2,
        [
            pltpu.VMEM((TOK, D), BF16),
            pltpu.VMEM((16, CHIP, 256), BF16),
            pltpu.VMEM((2, 128, 384), BF16),
            pltpu.VMEM((16, 256, 384), BF16),
            pltpu.VMEM((3, D, 64), BF16),
            pltpu.VMEM((16, 256, 192), BF16),
            pltpu.VMEM((192, 384), BF16),
            pltpu.VMEM((CHIP, 384), F32),
            DMA((10,)),
            DMA((16,)),
            DMA((20,)),
            DMA((4,)),
            DMA((4,)),
        ],
        1,
    )(
        activations,
        norm_gain.reshape(1, D),
        query_weight,
        key_weight,
        value_weight,
        query_down,
        key_down,
        value_down,
        query_up,
        key_up,
        value_up,
        jnp.asarray(tables),
        jnp.asarray(bases),
    )
    mixed, log_sums = call(
        attend_kernel,
        [half, ((CHIP, 128), F32)],
        [SMEM, VMEM, ANY, ANY],
        [
            pltpu.VMEM((16, TOK, 384), BF16),
            pltpu.VMEM((CHIP, 128), F32),
            pltpu.VMEM((CHIP, 256), F32),
            DMA((4,)),
            DMA((16,)),
            DMA((20,)),
        ],
        2,
    )(shifted, q, k, v)
    return call(
        output_kernel,
        [((TOK, 512), BF16), ((TOK, 2), F32)],
        [ANY, ANY, VMEM, VMEM, ANY],
        [
            pltpu.VMEM((16, 256, 256), BF16),
            pltpu.VMEM((2, TOK, 128), F32),
            pltpu.VMEM((64, 512), BF16),
            pltpu.VMEM((TOK, 64), F32),
            pltpu.VMEM((TOK, 512), F32),
            DMA((4,)),
            DMA((16,)),
            DMA((20,)),
            DMA,
        ],
        3,
    )(mixed, log_sums, columns, output_down.reshape(8, 256, 64), output_up_matrix)


def solution(mesh):
    placed = (
        P("seq", None),
        P(),
        P(),
        P("seq", "head"),
        P("seq", "head"),
        P("seq", "head"),
        P("head", "seq"),
        P(),
        P(),
        P(),
        P(),
        P(),
        P(),
        P(),
        P(),
    )
    return jax.shard_map(
        body,
        mesh=mesh,
        in_specs=placed,
        out_specs=(P("seq", "head"), P("seq", "head")),
        check_vma=False,
    )
```

time: 613 us -> 184 us (0.30)
  the two profiles are of different devices: /device:TPU:38 before, /device:TPU:12 now
where the time goes in v1:
time: 184 us; the launch traced here: 183 us
  Pallas kernels  143 us (78%)
  between operations  14.1 us (8%)
  local copies, waits for them, and re-layouts  12.2 us (7%)
  starting transfers between devices  8.65 us (5%)
  waiting for transfers between devices  5.28 us (3%)
    pallas_call x1, Pallas kernels, body(): call(project_kernel, [half, half, half], [ANY] + [VMEM] * 4 + [ANY] * 6 +...  54.9 us
    pallas_call x1, Pallas kernels, body(): call(attend_kernel, [half, ((CHIP, 128), F32)], [SMEM, VMEM, ANY, ANY], [...  52.9 us
    pallas_call x1, Pallas kernels, body(): call(output_kernel, [((TOK, 512), BF16), ((TOK, 2), F32)], [ANY, ANY, VME...  35.2 us
    unnamed x9, local copies, waits for them, and re-layouts  10.6 us
    ppermute x1, starting transfers between devices, body(): turned = lax.ppermute(output_weight, ('seq', 'head'), pairs)  8.61 us
    ppermute x1, waiting for transfers between devices, body(): turned = lax.ppermute(output_weight, ('seq', 'head'), pairs)  5.25 us
  transfers between devices with their start and end apart: 2, of which 1 were waited for; matrix products, arithmetic and copies ran while one was open for 4% of the time, Pallas kernels for 59%

profile of v1, /device:TPU:12, one launch (start us, length us, event | category | flops | bytes accessed | tf_op | source)
XLA Modules:
  0.0 183.2 jit_solution(2267797762702778223)
XLA Ops:
  7.2 0.0 copy-start
  7.2 0.0 all-gather.3.cloned.1.call-start
  7.2 8.6 %collective-permute-start = (bf16[256,128]{1,0:T(8,128)(2,1)}, bf16[256,128]{1,0:T(8,128)(2,1)S(1)}, u32[]{:S(2)}, u32[]{:S(2)}) collective-permute-start(bf16[256,128]{1,0:T(8,128)(2,1)} %param.23), channel_id=1, source_target_pairs={{0,0},{1,32},{2,64},{3,96},{4,128},{5,160},{6,192},{7,224},{8,8},{... | collective-permute-start | bytes 196616 | tf_op jit(solution)/shard_map/ppermute | solution.py:539
  15.8 5.2 %collective-permute-done = bf16[256,128]{1,0:T(8,128)(2,1)S(1)} collective-permute-done((bf16[256,128]{1,0:T(8,128)(2,1)}, bf16[256,128]{1,0:T(8,128)(2,1)S(1)}, u32[]{:S(2)}, u32[]{:S(2)}) %collective-permute-start) | collective-permute-done | bytes 65568 | tf_op jit(solution)/shard_map/ppermute | solution.py:539
  21.1 0.0 copy-start.1
  21.1 0.6 copy-done.1
  21.7 0.0 all-gather.3.cloned.1.call-update
  21.7 2.4 %copy.19.down_q = bf16[4096,64]{1,0:T(8,128)(2,1)} copy(bf16[4096,64]{0,1:T(8,128)(2,1)} %param.24) | data formatting | bytes 1048576 | tf_op args[7]
  24.1 2.4 %copy.20.down_k = bf16[4096,64]{1,0:T(8,128)(2,1)} copy(bf16[4096,64]{0,1:T(8,128)(2,1)} %param.26) | data formatting | bytes 1048576 | tf_op args[9]
  26.5 2.3 %copy.21.down_v = bf16[4096,64]{1,0:T(8,128)(2,1)} copy(bf16[4096,64]{0,1:T(8,128)(2,1)} %param.28) | data formatting | bytes 1048576 | tf_op args[11]
  28.8 0.0 copy-done
  28.8 1.0 copy.22
  29.8 54.9 %shard_map.176 = (bf16[1024,128]{1,0:T(8,128)(2,1)}, bf16[1024,128]{1,0:T(8,128)(2,1)}, bf16[1024,128]{1,0:T(8,128)(2,1)}) custom-call(bf16[512,4096]{1,0:T(8,128)(2,1)} %act.1, f32[1,4096]{1,0:T(1,128)} %bitcast.5, bf16[128,256]{1,0:T(8,128)(2,1)} %wq.1, bf16[128,256]{1,0:T(8,128)(2,1)} %wk.1, bf16[128,256]{1,0:T(8,128)(2,1)} %wv.1, ...), custom_call_target="tpu_custom_call" | custom-call | tf_op jit(solution)/shard_map/pallas_call | solution.py:544
  84.7 52.9 %shard_map.177 = (bf16[1024,128]{1,0:T(8,128)(2,1)}, f32[1024,128]{1,0:T(8,128)}) custom-call(s32[16]{0:T(128)} %shifted.1, bf16[1024,128]{1,0:T(8,128)(2,1)} %get-tuple-element.7.q, bf16[1024,128]{1,0:T(8,128)(2,1)} %get-tuple-element.8.k, bf16[1024,128]{1,0:T(8,128)(2,1)} %get-tuple-element.9.v), custom_call_target="tpu_custom_call" | custom-call | tf_op jit(solution)/shard_map/pallas_call | solution.py:579
  137.6 0.0 all-gather.3.cloned.1.call-done
  137.6 35.2 %shard_map.178 = (bf16[512,512]{1,0:T(8,128)(2,1)}, f32[512,2]{1,0:T(8,128)}) custom-call(bf16[1024,128]{1,0:T(8,128)(2,1)} %get-tuple-element.10.mixed, f32[1024,128]{1,0:T(8,128)} %get-tuple-element.11.log_sums, bf16[32,256,128]{2,1,0:T(8,128)(2,1)} %bitcast.4, bf16[8,256,64]{2,1,0:T(8,128)(2,1)} %bitcast.3, bf16[64,4096]{1,0:T(8,128)(2,1)} %up.1), custom_call_target="tpu_custom_call" | custom-call | tf_op jit(solution)/shard_map/pallas_call | solution.py:593
  172.8 1.7 copy.23
  174.5 1.9 %copy.25 = bf16[512,512]{1,0:T(8,128)(2,1)} copy(bf16[512,512]{1,0:T(8,128)(2,1)} %get-tuple-element.16) | data formatting | bytes 1048576
Async XLA Ops:
  7.2 21.7 %copy-start = (bf16[2048,64]{0,1:T(8,128)(2,1)S(1)}, bf16[2048,64]{0,1:T(8,128)(2,1)}, u32[]{:S(2)}) copy-start(bf16[2048,64]{0,1:T(8,128)(2,1)} %param.30) | copy-start | bytes 786436
  7.2 130.5 %all-gather.3.cloned.1.call-start = ((), (), s32[]{:S(2)}) async-start(), calls=%async_computation | async-start | bytes 2162688 | tf_op jit(solution)/shard_map/all_gather | solution.py:540
  7.2 13.9 %collective-permute-start = (bf16[256,128]{1,0:T(8,128)(2,1)}, bf16[256,128]{1,0:T(8,128)(2,1)S(1)}, u32[]{:S(2)}, u32[]{:S(2)}) collective-permute-start(bf16[256,128]{1,0:T(8,128)(2,1)} %param.23), channel_id=1, source_target_pairs={{0,0},{1,32},{2,64},{3,96},{4,128},{5,160},{6,192},{7,224},{8,8},{... | collective-permute-start | bytes 196616 | tf_op jit(solution)/shard_map/ppermute | solution.py:539
  21.1 0.6 copy-start.1
Sparse Core Ops, SparseCore 0:
  21.9 71.1 all-gather.2

commit v2 on v0

v2 whole, which is shorter than its diff:
```python
import math

import jax
import jax.numpy as jnp
import numpy as np
from jax import lax
from jax.experimental import pallas as pl
from jax.experimental.pallas import tpu as pltpu
from jax.sharding import PartitionSpec as P

EPS = 1e-05
ADAPTER_SCALING = 0.5
ROPE_BASE = 10000.0
MASKED = -1e30
D = 4096
HD = 128
TOK = 512
MESH = pl.DeviceIdType.MESH
F32 = jnp.float32
BF16 = jnp.bfloat16
VMEM_BYTES = 56 * 1024 * 1024


def spot():
    seq = lax.axis_index("seq")
    head = lax.axis_index("head")
    return seq // 8, (seq // 2) % 4, seq % 2, head // 2, head % 2


def seq_of(z, x, core):
    return z * 8 + x * 2 + core


def remote(source, target, send, receive, device):
    return pltpu.make_async_remote_copy(
        src_ref=source,
        dst_ref=target,
        send_sem=send,
        recv_sem=receive,
        device_id=device,
        device_id_type=MESH,
    )


def dot(a, b):
    return jnp.dot(a, b, preferred_element_type=F32)


def dot_nt(a, b):
    return lax.dot_general(a, b, (((1,), (1,)), ((), ())), preferred_element_type=F32)


def times(value, n):
    return jnp.concatenate([value] * n, axis=1)


class Ring:
    def __init__(self, views, receive, send, place, right, left, twin=None, sibling=None):
        self.view, self.other = views
        self.receive, self.send = receive, send
        self.place, self.right, self.left = place, right, left
        self.twin, self.sibling = twin, sibling
        self.open = []

    def slot(self, d, step):
        return d * 4 + (self.place + step) % 4

    def start(self, source, target, receive, device):
        copy = remote(source, target, self.send(len(self.open)), receive, device)
        copy.start()
        self.open.append(copy)

    def push(self, d, step, device):
        slot = self.slot(d, step)
        self.start(self.view(slot), self.view(slot), self.receive(slot), device)

    def push_far(self, d, step, far, device):
        slot, there = self.slot(d, step), self.slot(far, step)
        self.start(self.view(slot), self.view(there), self.receive(there), device)

    def push_own(self, d):
        self.push(d, 0, self.right)
        self.push(d, 0, self.left)

    def hand(self, d, step):
        if self.sibling is not None:
            slot = self.slot(d, step)
            self.start(self.view(slot), self.view(slot), self.twin(slot), self.sibling)

    def handed(self, d, step):
        slot = self.slot(d, step)
        ref = self.other(slot)
        remote(ref, ref, self.send(0), self.twin(slot), self.sibling).wait_recv()

    def arrived(self, d, step):
        slot = self.slot(d, step)
        ref = self.view(slot)
        remote(ref, ref, self.send(0), self.receive(slot), self.right).wait_recv()

    def own(self, d):
        self.arrived(d, 0)
        self.push_own(d)
        self.hand(d, 0)

    def from_left(self, d, forward=True):
        self.arrived(d, 3)
        if forward and d % 2 == 0:
            self.push(d, 3, self.right)
        self.hand(d, 3)

    def from_right(self, d, forward=True):
        self.arrived(d, 1)
        if forward and d % 2 == 1:
            self.push(d, 1, self.left)
        self.hand(d, 1)

    def across(self, d):
        self.arrived(d, 2)
        self.hand(d, 2)

    def finish(self):
        for copy in self.open:
            copy.wait_send()


INPUTS = [
    "act",
    "gain",
    "shifted",
    "wq",
    "wk",
    "wv",
    "wo",
    "down_q",
    "up_q",
    "down_k",
    "up_k",
    "down_v",
    "up_v",
    "down_o",
    "up_o",
    "tables",
    "bases",
]
OUTPUTS = ["out", "sums_out"]
DMA = pltpu.SemaphoreType.DMA
SCRATCH = dict(
    raw=pltpu.VMEM((TOK, D), BF16),
    normed=pltpu.VMEM((16, TOK, 256), BF16),
    weights=pltpu.VMEM((2, 16, 256, 384), BF16),
    down_all=pltpu.VMEM((192, D), BF16),
    up_all=pltpu.VMEM((2, 192, 384), BF16),
    total=pltpu.VMEM((2, TOK, 384), F32),
    q=pltpu.VMEM((2, TOK, HD), BF16),
    kv=pltpu.VMEM((2, 2, 16, 256, 384), BF16),
    top=pltpu.VMEM((TOK, 128), F32),
    mix=pltpu.VMEM((TOK, 256), F32),
    columns=pltpu.VMEM((32, 256, 128), BF16),
    held=pltpu.VMEM((2, 16, 256, 128), BF16),
    up_here=pltpu.VMEM((64, 512), BF16),
    low=pltpu.VMEM((TOK, 64), F32),
    result=pltpu.VMEM((TOK, 512), F32),
    load=DMA((15,)),
    weight_receive=DMA((2, 16)),
    weight_twin=DMA((2, 16)),
    weight_send=DMA((2, 31)),
    key_receive=DMA((2, 16)),
    key_twin=DMA((2, 16)),
    key_send=DMA((2, 30)),
    mix_receive=DMA((2, 16)),
    mix_send=DMA((2, 14)),
    column_receive=DMA((16,)),
    column_twin=DMA((16,)),
    column_send=DMA((32,)),
)


class Refs:
    pass


def kernel(*refs):
    r = Refs()
    for name, ref in zip(INPUTS + OUTPUTS + list(SCRATCH), refs):
        setattr(r, name, ref)
    z, x, core, y, zh = spot()
    seq = lax.axis_index("seq")
    head = lax.axis_index("head")
    sibling = (seq_of(z, x, 1 - core), head)
    right = (seq_of(z, (x + 1) % 4, core), head)
    left = (seq_of(z, (x + 3) % 4, core), head)
    planes = [(seq_of((z + e) % 4, x, core), head) for e in range(1, 4)]
    up_y = (seq, ((y + 1) % 4) * 2 + zh)
    down_y = (seq, ((y + 3) % 4) * 2 + zh)
    partner = (seq, y * 2 + 1 - zh)
    turn_seq = head * 4 + seq % 4
    turned = (turn_seq, seq // 4)
    stays = seq // 4 == head

    loads = []
    for part in range(4):
        rows = pl.ds(part * 128, 128)
        loads.append(pltpu.make_async_copy(r.act.at[rows], r.raw.at[rows], r.load.at[part]))
    for index, ref in enumerate((r.down_k, r.down_v, r.down_q)):
        target = r.down_all.at[pl.ds(index * 64, 64)]
        loads.append(pltpu.make_async_copy(ref, target, r.load.at[4 + index]))
    r.up_all[...] = jnp.zeros_like(r.up_all)
    for side in range(2):
        here = pl.ds(pl.multiple_of(head * 256 + side * 128, 128), 128)
        for index, ref in enumerate((r.up_k, r.up_v, r.up_q)):
            target = r.up_all.at[side, pl.ds(index * 64, 64), pl.ds(index * 128, 128)]
            loads.append(
                pltpu.make_async_copy(
                    ref.at[:, here], target, r.load.at[7 + side * 3 + index]
                )
            )
    source = r.up_o.at[:, pl.ds(pl.multiple_of(head * 512, 512), 512)]
    loads.append(pltpu.make_async_copy(source, r.up_here, r.load.at[13]))
    for copy in loads:
        copy.start()
    own_rows = pl.ds(pl.multiple_of(core * 128, 128), 128)
    other_rows = pl.ds(pl.multiple_of(128 - core * 128, 128), 128)
    for side in range(2):
        for index, ref in enumerate((r.wk, r.wv, r.wq)):
            r.weights[side, x, own_rows, index * 128 : index * 128 + 128] = ref[
                :, side * 128 : side * 128 + 128
            ]

    def ones(slot, carry):
        for side in range(2):
            for which in range(2):
                r.kv[side, which, slot, :, 256:384] = jnp.ones((256, 128), BF16)
        return carry

    lax.fori_loop(0, 16, ones, 0)

    barrier = pltpu.get_barrier_semaphore()
    everyone = [sibling, right, left, up_y, down_y, partner] + planes
    for device in everyone:
        pl.semaphore_signal(barrier, inc=1, device_id=device, device_id_type=MESH)

    @pl.when(jnp.logical_not(stays))
    def _():
        pl.semaphore_signal(barrier, inc=1, device_id=turned, device_id_type=MESH)

    pl.semaphore_wait(barrier, len(everyone) + 1 - stays.astype(jnp.int32))

    def weight_ring(side):
        return Ring(
            (
                lambda slot: r.weights.at[side, slot, own_rows],
                lambda slot: r.weights.at[side, slot, other_rows],
            ),
            lambda slot: r.weight_receive.at[side, slot],
            lambda index: r.weight_send.at[side, index],
            x, right, left,
            lambda slot: r.weight_twin.at[side, slot],
            sibling,
        )

    def key_ring(side):
        return Ring(
            (
                lambda slot: r.kv.at[side, core, slot, :, pl.ds(0, 256)],
                lambda slot: r.kv.at[side, 1 - core, slot, :, pl.ds(0, 256)],
            ),
            lambda slot: r.key_receive.at[side, slot],
            lambda index: r.key_send.at[side, index],
            x, right, left,
            lambda slot: r.key_twin.at[side, slot],
            sibling,
        )

    def mix_ring(side):
        return Ring(
            (lambda slot: r.held.at[side, slot], None),
            lambda slot: r.mix_receive.at[side, slot],
            lambda index: r.mix_send.at[side, index],
            y, up_y, down_y,
        )

    weights = [weight_ring(side) for side in range(2)]
    keys = [key_ring(side) for side in range(2)]
    mixes = [mix_ring(side) for side in range(2)]
    columns = Ring(
        (
            lambda slot: r.columns.at[core * 16 + slot],
            lambda slot: r.columns.at[(1 - core) * 16 + slot],
        ),
        lambda slot: r.column_receive.at[slot],
        lambda index: r.column_send.at[index],
        x, right, left,
        lambda slot: r.column_twin.at[slot],
        sibling,
    )

    def to_planes(ring):
        for e, device in zip(range(1, 4), planes):
            ring.push_far(0, 0, e, device)

    def turn_copy():
        place = (turn_seq // 2) % 4
        return remote(
            r.wo,
            r.columns.at[(turn_seq % 2) * 16 + place],
            r.column_send.at[31],
            r.column_receive.at[place],
            turned,
        )

    def normalize(part):
        loads[part].wait()

        def tile(index, carry):
            row = part * 128 + index * 16
            wide = r.raw[pl.ds(row, 16), :].astype(F32)
            mean_square = jnp.mean(wide * wide, axis=-1, keepdims=True)
            value = (wide * lax.rsqrt(mean_square + EPS) * r.gain[...]).astype(BF16)
            for chunk in range(16):
                r.normed[chunk, pl.ds(row, 16), :] = value[:, chunk * 256 : chunk * 256 + 256]
            return carry

        lax.fori_loop(0, 8, tile, 0)

    def reduced():
        def block(index, carry):
            rows = pl.ds(pl.multiple_of(index * 256, 256), 256)
            value = jnp.zeros((256, 192), F32)
            for chunk in range(16):
                value = value + dot_nt(
                    r.normed[chunk, rows, :], r.down_all[:, chunk * 256 : chunk * 256 + 256]
                )
            value = value.astype(BF16)
            for side in range(2):
                r.total[side, rows, :] = ADAPTER_SCALING * dot(value, r.up_all[side])
            return carry

        lax.fori_loop(0, 2, block, 0)

    def accumulate(side, d):
        ring = weights[side]
        for step in range(4):
            ring.handed(d, step)

        def block(index, carry):
            rows = pl.ds(pl.multiple_of(index * 256, 256), 256)
            value = r.total[side, rows, :]
            for step in range(4):
                chunk = ((z + 4 - d) % 4) * 4 + (x + step) % 4
                value = value + dot(
                    r.normed[chunk, rows, :], r.weights[side, ring.slot(d, step)]
                )
            r.total[side, rows, :] = value
            return carry

        lax.fori_loop(0, 2, block, 0)

    base = r.bases[pl.ds(seq, 1)]
    base_cos, base_sin = base[0, 0:1, :], base[0, 1:2, :]

    def project(side):
        ring = keys[side]
        for part in range(2):
            slot = ring.slot(part, 0)

            def tile(index, carry):
                rows = pl.ds(pl.multiple_of(part * 256 + index * 128, 128), 128)
                there = pl.ds(pl.multiple_of(index * 128, 128), 128)
                cos_row, sin_row = r.tables[0, rows, :], r.tables[1, rows, :]
                cos = cos_row * base_cos - sin_row * base_sin
                sin = sin_row * base_cos + cos_row * base_sin
                key = r.total[side, rows, 0:128]
                key = key * cos + pltpu.roll(key, 64, 1) * sin
                r.kv[side, core, slot, there, 0:128] = key.astype(BF16)
                r.kv[side, core, slot, there, 128:256] = r.total[side, rows, 128:256].astype(BF16)
                query = r.total[side, rows, 256:384]
                query = query * cos + pltpu.roll(query, 64, 1) * sin
                query = query * (math.log2(math.e) / math.sqrt(HD))
                r.q[side, rows, :] = query.astype(BF16)
                return carry

            lax.fori_loop(0, 2, tile, 0)
            ring.push_own(part)
            ring.push_far(part, 0, part + 2, planes[0])
            ring.hand(part, 0)

    def diagonal(side):
        for index in range(2):
            rows = pl.ds(index * 256, 256)
            pieces = []
            for part in range(index + 1):
                slot = keys[side].slot(part, 0)
                scores = dot_nt(r.q[side, rows, :], r.kv[side, core, slot, :, 0:128])
                if part == index:
                    row = lax.broadcasted_iota(jnp.int32, scores.shape, 0)
                    column = lax.broadcasted_iota(jnp.int32, scores.shape, 1)
                    scores = jnp.where(column <= row, scores, MASKED)
                pieces.append((slot, scores))
            highest = jnp.max(pieces[0][1], axis=1, keepdims=True)
            for slot, scores in pieces[1:]:
                highest = jnp.maximum(highest, jnp.max(scores, axis=1, keepdims=True))
            highest = jnp.broadcast_to(highest, (256, 128))
            value = jnp.zeros((256, 256), F32)
            for slot, scores in pieces:
                soft = jnp.exp2(scores - times(highest, 2)).astype(BF16)
                value = value + dot(soft, r.kv[side, core, slot, :, 128:384])
            r.top[rows, :] = highest
            r.mix[rows, :] = value

    def attend(side, places, bias):
        def block(index, carry):
            rows = pl.ds(pl.multiple_of(index * 256, 256), 256)
            query = r.q[side, rows, :]
            scores = [dot_nt(query, r.kv[side, which, slot, :, 0:128]) for which, slot in places]
            highest = scores[0]
            for value in scores[1:]:
                highest = jnp.maximum(highest, value)
            highest = jnp.max(highest, axis=1, keepdims=True)
            old = r.top[rows, :]
            new = jnp.maximum(old, highest + bias)
            level = times(new - bias, 2)
            value = r.mix[rows, :] * times(jnp.exp2(old - new), 2)
            for score, (which, slot) in zip(scores, places):
                soft = jnp.exp2(score - level).astype(BF16)
                value = value + dot(soft, r.kv[side, which, slot, :, 128:384])
            r.top[rows, :] = new
            r.mix[rows, :] = value
            return carry

        lax.fori_loop(0, 2, block, 0)

    def chip_places(side, d, step):
        slots = [keys[side].slot(d + part, step) for part in range(2)]
        return [(which, slot) for which in range(2) for slot in slots]

    def near(side):
        ring = keys[side]
        for part in range(2):
            ring.handed(part, 0)

        @pl.when(core == 1)
        def _():
            attend(side, [(0, ring.slot(part, 0)) for part in range(2)], 0.0)

    def own_plane(side, step):
        for part in range(2):
            keys[side].handed(part, step)

        @pl.when((x + step) % 4 < x)
        def _():
            attend(side, chip_places(side, 0, step), 0.0)

    def plane_before(side, step):
        for part in range(2):
            keys[side].handed(part + 2, step)
        flag = r.shifted[head * 2 + side]
        reaches = (z % 2) * (1 - flag) + (1 - z % 2) * flag
        bias = (reaches.astype(F32) - 1.0) * (-MASKED)
        attend(side, chip_places(side, 2, step), bias)

    def pass_on(side, d):
        keys[side].across(d)
        keys[side].push_far(d, 2, d + 2, planes[0])

    def close(side):
        ring = mixes[side]
        for part in range(2):
            rows = pl.ds(part * 256, 256)
            weight = r.mix[rows, 128:256]
            r.held[side, ring.slot(part, 0)] = (r.mix[rows, 0:128] / weight).astype(BF16)
            ring.push_far(part, 0, part + 2, partner)
            ring.push_own(part)
        for part in range(4):
            rows = pl.ds(part * 128, 128)
            sums = (r.top[rows, :] + jnp.log2(r.mix[rows, 128:256])) * math.log(2.0)
            r.sums_out[side : side + 1, part * 128 : part * 128 + 128] = sums.T[0:1, :]

    def add(side, d, step):
        rows = pl.ds((d % 2) * 256, 256)
        group = ((y + step) % 4) * 2 + (zh + d // 2) % 2
        block = r.held[side, mixes[side].slot(d, step)]
        behind = (z + 4 - group // 2) % 4
        first = behind * 4 + (group % 2) * 2
        rows_in = slice(side * 128, side * 128 + 128)
        matrix = jnp.concatenate(
            [r.columns[(j % 2) * 16 + first + j // 2, rows_in, :] for j in range(4)], axis=1
        )
        r.result[rows, :] += dot(block, matrix)
        lanes = pl.ds(pl.multiple_of(group * 256 + side * 128, 128), 128)
        r.low[rows, :] += dot_nt(block, r.down_o[:, lanes])

    w0, w1 = weights
    k0, k1 = keys
    m0, m1 = mixes
    to_planes(w0)
    w0.push_own(0)
    w0.hand(0, 0)

    @pl.when(jnp.logical_not(stays))
    def _():
        turn_copy().start()

    @pl.when(stays)
    def _():
        copy = pltpu.make_async_copy(
            r.wo, r.columns.at[(turn_seq % 2) * 16 + (turn_seq // 2) % 4], r.load.at[14]
        )
        copy.start()
        copy.wait()

    normalize(0)
    normalize(1)
    w0.own(1)
    w0.from_left(0)
    w0.from_right(0)
    normalize(2)
    normalize(3)
    w0.own(2)
    for copy in loads[4:]:
        copy.wait()
    reduced()
    w0.from_left(1)
    w0.from_right(1)
    w0.own(3)
    w0.across(0)
    accumulate(0, 0)
    to_planes(w1)
    w0.from_left(2)
    w0.from_right(2)
    w0.across(1)
    accumulate(0, 1)
    w0.from_left(3)
    w0.from_right(3)
    w1.push_own(0)
    w1.hand(0, 0)
    w1.own(1)
    w0.across(2)
    accumulate(0, 2)
    w1.own(2)
    w1.own(3)
    w0.across(3)
    accumulate(0, 3)
    project(0)

    for d in range(2):
        w1.from_left(d)
        w1.from_right(d)
    w1.across(0)
    accumulate(1, 0)
    for d in range(2, 4):
        w1.from_left(d)
        w1.from_right(d)
    w1.across(1)
    accumulate(1, 1)
    k0.from_left(0)
    k0.from_right(1)
    w1.across(2)
    accumulate(1, 2)
    w1.across(3)
    accumulate(1, 3)
    project(1)
    k0.from_left(1)
    k0.from_right(0)
    k0.own(2)
    k0.own(3)
    diagonal(0)
    near(0)
    own_plane(0, 3)
    pass_on(0, 0)
    pass_on(0, 1)
    k1.from_left(0)
    k1.from_right(1)
    own_plane(0, 1)
    plane_before(0, 0)
    own_plane(0, 2)
    k1.from_left(1)
    k1.from_right(0)
    k1.own(2)
    k1.own(3)
    for d in range(2, 4):
        k0.from_left(d, False)
        k0.from_right(d, False)
    plane_before(0, 3)
    plane_before(0, 1)
    pass_on(1, 0)
    pass_on(1, 1)
    k0.across(2)
    k0.across(3)
    plane_before(0, 2)
    close(0)

    @pl.when(jnp.logical_not(stays))
    def _():
        columns.arrived(0, 0)

    to_planes(columns)
    columns.hand(0, 0)
    diagonal(1)
    near(1)
    own_plane(1, 3)
    own_plane(1, 1)
    for d in range(2):
        m0.from_left(d)
        m0.from_right(d)
    own_plane(1, 2)
    plane_before(1, 0)
    columns.push_own(0)
    for d in range(1, 4):
        columns.own(d)
    for d in range(2, 4):
        k1.from_left(d, False)
        k1.from_right(d, False)
    m0.own(2)
    m0.own(3)
    plane_before(1, 3)
    plane_before(1, 1)
    k1.across(2)
    k1.across(3)
    plane_before(1, 2)
    close(1)

    for d in range(4):
        columns.from_left(d)
        columns.from_right(d)
    for d in range(2, 4):
        m0.from_left(d)
        m0.from_right(d)
    for d in range(2):
        m1.from_left(d)
        m1.from_right(d)
    for d in range(4):
        columns.across(d)
    r.result[...] = jnp.zeros_like(r.result)
    r.low[...] = jnp.zeros_like(r.low)
    for d in range(4):
        m0.across(d)
    m1.own(2)
    m1.own(3)
    for d in range(4):
        for step in range(4):
            columns.handed(d, step)
    for d in range(4):
        for step in range(4):
            add(0, d, step)
    for d in range(2):
        for step in (0, 1, 3):
            add(1, d, step)
    for d in range(2, 4):
        m1.from_left(d)
        m1.from_right(d)
    for d in range(2):
        m1.across(d)
        add(1, d, 2)
    for d in range(2, 4):
        for step in (0, 1, 3):
            add(1, d, step)
    for d in range(2, 4):
        m1.across(d)
        add(1, d, 2)
    r.out[...] = (
        r.result[...] + ADAPTER_SCALING * dot(r.low[...].astype(BF16), r.up_here[...])
    ).astype(BF16)
    for ring in weights + keys + mixes + [columns]:
        ring.finish()

    @pl.when(jnp.logical_not(stays))
    def _():
        turn_copy().wait_send()


def rope_tables():
    frequency = ROPE_BASE ** (-2.0 * np.arange(64, dtype=np.float64) / HD)
    sign = np.concatenate([-np.ones(64), np.ones(64)])

    def table(positions):
        angles = positions[:, None] * np.concatenate([frequency, frequency])[None, :]
        return np.cos(angles), np.sin(angles) * sign

    tables = np.stack(table(np.arange(TOK, dtype=np.float64)))
    bases = np.stack(table(np.arange(32, dtype=np.float64) * TOK), axis=1)
    return tables.astype(np.float32), bases.astype(np.float32)


VMEM = pl.BlockSpec(memory_space=pltpu.VMEM)
ANY = pl.BlockSpec(memory_space=pl.ANY)
SMEM = pl.BlockSpec(memory_space=pltpu.SMEM)


def body(
    activations,
    norm_gain,
    shifted,
    query_weight,
    key_weight,
    value_weight,
    output_weight,
    query_down,
    query_up,
    key_down,
    key_up,
    value_down,
    value_up,
    output_down,
    output_up_matrix,
):
    tables, bases = rope_tables()
    arguments = dict(
        act=(activations, ANY),
        gain=(norm_gain.reshape(1, D), VMEM),
        shifted=(shifted, SMEM),
        wq=(query_weight, VMEM),
        wk=(key_weight, VMEM),
        wv=(value_weight, VMEM),
        wo=(output_weight, VMEM),
        down_q=(query_down.T, ANY),
        up_q=(query_up, ANY),
        down_k=(key_down.T, ANY),
        up_k=(key_up, ANY),
        down_v=(value_down.T, ANY),
        up_v=(value_up, ANY),
        down_o=(output_down.T, VMEM),
        up_o=(output_up_matrix, ANY),
        tables=(jnp.asarray(tables), VMEM),
        bases=(jnp.asarray(bases), VMEM),
    )
    out, sums = pl.pallas_call(
        kernel,
        out_shape=(
            jax.ShapeDtypeStruct((TOK, 512), BF16),
            jax.ShapeDtypeStruct((2, TOK), F32),
        ),
        in_specs=[arguments[name][1] for name in INPUTS],
        out_specs=(VMEM, VMEM),
        scratch_shapes=list(SCRATCH.values()),
        compiler_params=pltpu.CompilerParams(
            collective_id=1, has_side_effects=True, vmem_limit_bytes=VMEM_BYTES
        ),
    )(*[arguments[name][0] for name in INPUTS])
    return out, sums.T


def solution(mesh):
    placed = (
        P("seq", None),
        P(),
        P(),
        P("seq", "head"),
        P("seq", "head"),
        P("seq", "head"),
        P("head", "seq"),
        P(),
        P(),
        P(),
        P(),
        P(),
        P(),
        P(),
        P(),
    )
    return jax.shard_map(
        body,
        mesh=mesh,
        in_specs=placed,
        out_specs=(P("seq", "head"), P("seq", "head")),
        check_vma=False,
    )
```

time: 613 us -> 132 us (0.22)
  waiting for transfers between devices: 393 us -> 0 us
  Pallas kernels: 0 us -> 128 us
  starting transfers between devices: 81.7 us -> 0 us
  matrix products: 76.6 us -> 0 us
  other arithmetic: 27.2 us -> 0 us
  local copies, waits for them, and re-layouts: 17.7 us -> 3.13 us
  between operations: 14.1 us -> 0.65 us
    reduce_scatter x1 -> x0, waiting for transfers between devices: 168 us -> none  [body(): lax.psum_scatter(summand_terms.astype(jnp.bfloat16), 'head', scatter_dime...]
    all_gather x4 -> x0, waiting for transfers between devices: 154 us -> none  [the longest x1 53 us: body(): lax.all_gather(query_weight, 'seq', axis=0, tiled=True)]
    pallas_call x0 -> x1, Pallas kernels: none -> 128 us  [body(): pl.pallas_call(kernel, out_shape=(jax.ShapeDtypeStruct((TOK, 512), BF16),...]
    ppermute x15 -> x0, starting transfers between devices: 81.5 us -> none  [from_behind(): return lax.ppermute(value, axis, pairs)]
    dot_general x40 -> x0, matrix products: 76.6 us -> none  [the longest x16 24.8 us: one_block(): jnp.einsum('hqk,khd->hqd', weights.astype(jnp.bfloat16), value_tile, pref...]
    ppermute x15 -> x0, waiting for transfers between devices: 68.9 us -> none  [from_behind(): return lax.ppermute(value, axis, pairs)]
    while x91 -> x0, local copies, waits for them, and re-layouts: 16.1 us -> none
    reduce_sum x17 -> x0, other arithmetic: 16.1 us -> none  [the longest x16 13 us: one_block(): new_sum = running_sum * rescale + jnp.sum(weights, axis=2)]
  transfers between devices with their start and end apart: 20 -> 0, of which waited for: 19 -> 0; matrix products, arithmetic and copies ran while one was open for 18% -> 0% of each run, Pallas kernels for 0% -> 0%
where the time goes in v2:
time: 132 us
  Pallas kernels  128 us (97%)
  local copies, waits for them, and re-layouts  3.13 us (2%)
    pallas_call x1, Pallas kernels, body(): pl.pallas_call(kernel, out_shape=(jax.ShapeDtypeStruct((TOK, 512), BF16),...  128 us
    unnamed x2, local copies, waits for them, and re-layouts  3.13 us

profile of v2, /device:TPU:38, one launch (start us, length us, event | category | flops | bytes accessed | tf_op | source)
XLA Modules:
  0.0 131.5 jit_solution(16274657183227099591)
XLA Ops:
  0.6 127.7 %shard_map.176 = (bf16[512,512]{1,0:T(8,128)(2,1)}, f32[2,512]{1,0:T(2,128)}) custom-call(bf16[512,4096]{1,0:T(8,128)(2,1)} %refs_0_.1, f32[1,4096]{1,0:T(1,128)} %bitcast.10, s32[16]{0:T(128)} %refs_2_.1, bf16[128,256]{1,0:T(8,128)(2,1)} %refs_3_.1, bf16[128,256]{1,0:T(8,128)(2,1)} %refs_4_.1, bf16[128,256]{1,0:T(8,128)(2,1)} %refs_5_.1, ...), custom_call_target="tpu_custom_call" | custom-call | tf_op jit(solution)/shard_map/pallas_call | solution.py:726
  128.4 1.9 %copy.21 = bf16[512,512]{1,0:T(8,128)(2,1)} copy(bf16[512,512]{1,0:T(8,128)(2,1)} %get-tuple-element.8) | data formatting | bytes 1048576
  130.3 1.3 copy.22

commit v3 on v2

--- a/solution.py
+++ b/solution.py
@@ -147,10 +147,12 @@
 SCRATCH = dict(
     raw=pltpu.VMEM((TOK, D), BF16),
     normed=pltpu.VMEM((16, TOK, 256), BF16),
-    weights=pltpu.VMEM((2, 16, 256, 384), BF16),
+    weights=pltpu.VMEM((16, 256, 768), BF16),
     down_all=pltpu.VMEM((192, D), BF16),
-    up_all=pltpu.VMEM((2, 192, 384), BF16),
-    total=pltpu.VMEM((2, TOK, 384), F32),
+    up_all=pltpu.VMEM((192, 768), BF16),
+    total=pltpu.VMEM((TOK, 768), F32),
+    tables_here=pltpu.VMEM((2, TOK, HD), F32),
+    down_here=pltpu.VMEM((64, 2048), BF16),
     q=pltpu.VMEM((2, TOK, HD), BF16),
     kv=pltpu.VMEM((2, 2, 16, 256, 384), BF16),
     top=pltpu.VMEM((TOK, 128), F32),
@@ -160,10 +162,10 @@
     up_here=pltpu.VMEM((64, 512), BF16),
     low=pltpu.VMEM((TOK, 64), F32),
     result=pltpu.VMEM((TOK, 512), F32),
-    load=DMA((15,)),
-    weight_receive=DMA((2, 16)),
-    weight_twin=DMA((2, 16)),
-    weight_send=DMA((2, 31)),
+    load=DMA((23,)),
+    weight_receive=DMA((3, 16)),
+    weight_twin=DMA((3, 16)),
+    weight_send=DMA((3, 31)),
     key_receive=DMA((2, 16)),
     key_twin=DMA((2, 16)),
     key_send=DMA((2, 30)),
@@ -197,34 +199,45 @@
     turned = (turn_seq, seq // 4)
     stays = seq // 4 == head
 
+    across_y = (seq, ((y + 2) % 4) * 2 + zh)
+    barrier = pltpu.get_barrier_semaphore()
+    everyone = [sibling, right, left, up_y, down_y, across_y, partner] + planes
+    for device in everyone:
+        pl.semaphore_signal(barrier, inc=1, device_id=device, device_id_type=MESH)
+
+    @pl.when(jnp.logical_not(stays))
+    def _():
+        pl.semaphore_signal(barrier, inc=1, device_id=turned, device_id_type=MESH)
+
+    own_rows = pl.ds(pl.multiple_of(core * 128, 128), 128)
+    other_rows = pl.ds(pl.multiple_of(128 - core * 128, 128), 128)
     loads = []
+
+    def load(source, target):
+        copy = pltpu.make_async_copy(source, target, r.load.at[len(loads)])
+        copy.start()
+        loads.append(copy)
+
+    places = {(0, 0): 0, (0, 1): 128, (1, 0): 256, (1, 1): 384, (0, 2): 512, (1, 2): 640}
+    for (side, index), place in places.items():
+        ref = (r.wk, r.wv, r.wq)[index]
+        load(
+            ref.at[:, pl.ds(side * 128, 128)],
+            r.weights.at[x, own_rows, pl.ds(place, 128)],
+        )
     for part in range(4):
         rows = pl.ds(part * 128, 128)
-        loads.append(pltpu.make_async_copy(r.act.at[rows], r.raw.at[rows], r.load.at[part]))
+        load(r.act.at[rows], r.raw.at[rows])
+    r.up_all[...] = jnp.zeros_like(r.up_all)
     for index, ref in enumerate((r.down_k, r.down_v, r.down_q)):
-        target = r.down_all.at[pl.ds(index * 64, 64)]
-        loads.append(pltpu.make_async_copy(ref, target, r.load.at[4 + index]))
-    r.up_all[...] = jnp.zeros_like(r.up_all)
-    for side in range(2):
+        load(ref, r.down_all.at[pl.ds(index * 64, 64)])
+    for (side, index), place in places.items():
         here = pl.ds(pl.multiple_of(head * 256 + side * 128, 128), 128)
-        for index, ref in enumerate((r.up_k, r.up_v, r.up_q)):
-            target = r.up_all.at[side, pl.ds(index * 64, 64), pl.ds(index * 128, 128)]
-            loads.append(
-                pltpu.make_async_copy(
-                    ref.at[:, here], target, r.load.at[7 + side * 3 + index]
-                )
-            )
-    source = r.up_o.at[:, pl.ds(pl.multiple_of(head * 512, 512), 512)]
-    loads.append(pltpu.make_async_copy(source, r.up_here, r.load.at[13]))
-    for copy in loads:
-        copy.start()
-    own_rows = pl.ds(pl.multiple_of(core * 128, 128), 128)
-    other_rows = pl.ds(pl.multiple_of(128 - core * 128, 128), 128)
-    for side in range(2):
-        for index, ref in enumerate((r.wk, r.wv, r.wq)):
-            r.weights[side, x, own_rows, index * 128 : index * 128 + 128] = ref[
-                :, side * 128 : side * 128 + 128
-            ]
+        ref = (r.up_k, r.up_v, r.up_q)[index]
+        load(ref.at[:, here], r.up_all.at[pl.ds(index * 64, 64), pl.ds(place, 128)])
+    load(r.tables, r.tables_here)
+    load(r.up_o.at[:, pl.ds(pl.multiple_of(head * 512, 512), 512)], r.up_here)
+    load(r.down_o, r.down_here)
 
     def ones(slot, carry):
         for side in range(2):
@@ -234,22 +247,30 @@
 
     lax.fori_loop(0, 16, ones, 0)
 
-    barrier = pltpu.get_barrier_semaphore()
-    everyone = [sibling, right, left, up_y, down_y, partner] + planes
-    for device in everyone:
-        pl.semaphore_signal(barrier, inc=1, device_id=device, device_id_type=MESH)
-
-    @pl.when(jnp.logical_not(stays))
-    def _():
-        pl.semaphore_signal(barrier, inc=1, device_id=turned, device_id_type=MESH)
-
+    def normalize(part):
+        loads[6 + part].wait()
+
+        def tile(index, carry):
+            row = part * 128 + index * 16
+            wide = r.raw[pl.ds(row, 16), :].astype(F32)
+            mean_square = jnp.mean(wide * wide, axis=-1, keepdims=True)
+            value = (wide * lax.rsqrt(mean_square + EPS) * r.gain[...]).astype(BF16)
+            for chunk in range(16):
+                r.normed[chunk, pl.ds(row, 16), :] = value[:, chunk * 256 : chunk * 256 + 256]
+            return carry
+
+        lax.fori_loop(0, 8, tile, 0)
+
+    normalize(0)
+    for copy in loads[:6]:
+        copy.wait()
     pl.semaphore_wait(barrier, len(everyone) + 1 - stays.astype(jnp.int32))
 
     def weight_ring(side):
         return Ring(
             (
-                lambda slot: r.weights.at[side, slot, own_rows],
-                lambda slot: r.weights.at[side, slot, other_rows],
+                lambda slot: r.weights.at[slot, own_rows, pl.ds(side * 256, 256)],
+                lambda slot: r.weights.at[slot, other_rows, pl.ds(side * 256, 256)],
             ),
             lambda slot: r.weight_receive.at[side, slot],
             lambda index: r.weight_send.at[side, index],
@@ -279,7 +300,7 @@
             y, up_y, down_y,
         )
 
-    weights = [weight_ring(side) for side in range(2)]
+    weights = [weight_ring(side) for side in range(3)]
     keys = [key_ring(side) for side in range(2)]
     mixes = [mix_ring(side) for side in range(2)]
     columns = Ring(
@@ -308,81 +329,51 @@
             turned,
         )
 
-    def normalize(part):
-        loads[part].wait()
-
-        def tile(index, carry):
-            row = part * 128 + index * 16
-            wide = r.raw[pl.ds(row, 16), :].astype(F32)
-            mean_square = jnp.mean(wide * wide, axis=-1, keepdims=True)
-            value = (wide * lax.rsqrt(mean_square + EPS) * r.gain[...]).astype(BF16)
-            for chunk in range(16):
-                r.normed[chunk, pl.ds(row, 16), :] = value[:, chunk * 256 : chunk * 256 + 256]
-            return carry
-
-        lax.fori_loop(0, 8, tile, 0)
-
     def reduced():
-        def block(index, carry):
-            rows = pl.ds(pl.multiple_of(index * 256, 256), 256)
-            value = jnp.zeros((256, 192), F32)
-            for chunk in range(16):
-                value = value + dot_nt(
-                    r.normed[chunk, rows, :], r.down_all[:, chunk * 256 : chunk * 256 + 256]
-                )
-            value = value.astype(BF16)
-            for side in range(2):
-                r.total[side, rows, :] = ADAPTER_SCALING * dot(value, r.up_all[side])
-            return carry
-
-        lax.fori_loop(0, 2, block, 0)
+        every = jnp.concatenate([r.normed[chunk] for chunk in range(16)], axis=1)
+        value = dot_nt(every, r.down_all[...]).astype(BF16)
+        r.total[...] = ADAPTER_SCALING * dot(value, r.up_all[...])
 
     def accumulate(side, d):
         ring = weights[side]
         for step in range(4):
             ring.handed(d, step)
-
-        def block(index, carry):
-            rows = pl.ds(pl.multiple_of(index * 256, 256), 256)
-            value = r.total[side, rows, :]
-            for step in range(4):
-                chunk = ((z + 4 - d) % 4) * 4 + (x + step) % 4
-                value = value + dot(
-                    r.normed[chunk, rows, :], r.weights[side, ring.slot(d, step)]
-                )
-            r.total[side, rows, :] = value
-            return carry
-
-        lax.fori_loop(0, 2, block, 0)
+        chunks = [((z + 4 - d) % 4) * 4 + (x + step) % 4 for step in range(4)]
+        left_side = jnp.concatenate([r.normed[chunk] for chunk in chunks], axis=1)
+        lanes = slice(side * 256, side * 256 + 256)
+        matrix = jnp.concatenate(
+            [r.weights[ring.slot(d, step), :, lanes] for step in range(4)], axis=0
+        )
+        r.total[:, lanes] += dot(left_side, matrix)
 
     base = r.bases[pl.ds(seq, 1)]
     base_cos, base_sin = base[0, 0:1, :], base[0, 1:2, :]
 
-    def project(side):
+    def turned_rows(rows, value):
+        cos_row, sin_row = r.tables_here[0, rows, :], r.tables_here[1, rows, :]
+        cos = cos_row * base_cos - sin_row * base_sin
+        sin = sin_row * base_cos + cos_row * base_sin
+        return value * cos + pltpu.roll(value, 64, 1) * sin
+
+    def project_keys(side):
         ring = keys[side]
         for part in range(2):
             slot = ring.slot(part, 0)
-
-            def tile(index, carry):
-                rows = pl.ds(pl.multiple_of(part * 256 + index * 128, 128), 128)
-                there = pl.ds(pl.multiple_of(index * 128, 128), 128)
-                cos_row, sin_row = r.tables[0, rows, :], r.tables[1, rows, :]
-                cos = cos_row * base_cos - sin_row * base_sin
-                sin = sin_row * base_cos + cos_row * base_sin
-                key = r.total[side, rows, 0:128]
-                key = key * cos + pltpu.roll(key, 64, 1) * sin
-                r.kv[side, core, slot, there, 0:128] = key.astype(BF16)
-                r.kv[side, core, slot, there, 128:256] = r.total[side, rows, 128:256].astype(BF16)
-                query = r.total[side, rows, 256:384]
-                query = query * cos + pltpu.roll(query, 64, 1) * sin
-                query = query * (math.log2(math.e) / math.sqrt(HD))
-                r.q[side, rows, :] = query.astype(BF16)
-                return carry
-
-            lax.fori_loop(0, 2, tile, 0)
+            rows = pl.ds(part * 256, 256)
+            key = turned_rows(rows, r.total[rows, side * 256 : side * 256 + 128])
+            r.kv[side, core, slot, :, 0:128] = key.astype(BF16)
+            value = r.total[rows, side * 256 + 128 : side * 256 + 256]
+            r.kv[side, core, slot, :, 128:256] = value.astype(BF16)
             ring.push_own(part)
             ring.push_far(part, 0, part + 2, planes[0])
             ring.hand(part, 0)
+
+    def project_queries(side):
+        for part in range(4):
+            rows = pl.ds(part * 128, 128)
+            query = turned_rows(rows, r.total[rows, 512 + side * 128 : 640 + side * 128])
+            query = query * (math.log2(math.e) / math.sqrt(HD))
+            r.q[side, rows, :] = query.astype(BF16)
 
     def diagonal(side):
         for index in range(2):
@@ -408,26 +399,18 @@
             r.mix[rows, :] = value
 
     def attend(side, places, bias):
-        def block(index, carry):
-            rows = pl.ds(pl.multiple_of(index * 256, 256), 256)
-            query = r.q[side, rows, :]
-            scores = [dot_nt(query, r.kv[side, which, slot, :, 0:128]) for which, slot in places]
-            highest = scores[0]
-            for value in scores[1:]:
-                highest = jnp.maximum(highest, value)
-            highest = jnp.max(highest, axis=1, keepdims=True)
+        key = jnp.concatenate([r.kv[side, which, slot, :, 0:128] for which, slot in places], axis=0)
+        value = jnp.concatenate(
+            [r.kv[side, which, slot, :, 128:384] for which, slot in places], axis=0
+        )
+        for index in range(4):
+            rows = pl.ds(index * 128, 128)
+            scores = dot_nt(r.q[side, rows, :], key)
             old = r.top[rows, :]
-            new = jnp.maximum(old, highest + bias)
-            level = times(new - bias, 2)
-            value = r.mix[rows, :] * times(jnp.exp2(old - new), 2)
-            for score, (which, slot) in zip(scores, places):
-                soft = jnp.exp2(score - level).astype(BF16)
-                value = value + dot(soft, r.kv[side, which, slot, :, 128:384])
+            new = jnp.maximum(old, jnp.max(scores, axis=1, keepdims=True) + bias)
+            soft = jnp.exp2(scores - times(new - bias, 2 * len(places))).astype(BF16)
+            r.mix[rows, :] = r.mix[rows, :] * times(jnp.exp2(old - new), 2) + dot(soft, value)
             r.top[rows, :] = new
-            r.mix[rows, :] = value
-            return carry
-
-        lax.fori_loop(0, 2, block, 0)
 
     def chip_places(side, d, step):
         slots = [keys[side].slot(d + part, step) for part in range(2)]
@@ -462,6 +445,10 @@
         keys[side].across(d)
         keys[side].push_far(d, 2, d + 2, planes[0])
 
+    def push_mixed(side, d):
+        for device in (up_y, down_y, across_y):
+            mixes[side].push(d, 0, device)
+
     def close(side):
         ring = mixes[side]
         for part in range(2):
@@ -469,32 +456,66 @@
             weight = r.mix[rows, 128:256]
             r.held[side, ring.slot(part, 0)] = (r.mix[rows, 0:128] / weight).astype(BF16)
             ring.push_far(part, 0, part + 2, partner)
-            ring.push_own(part)
+        for part in range(2):
+            push_mixed(side, part)
         for part in range(4):
             rows = pl.ds(part * 128, 128)
             sums = (r.top[rows, :] + jnp.log2(r.mix[rows, 128:256])) * math.log(2.0)
             r.sums_out[side : side + 1, part * 128 : part * 128 + 128] = sums.T[0:1, :]
 
-    def add(side, d, step):
+    def add(side, d):
         rows = pl.ds((d % 2) * 256, 256)
-        group = ((y + step) % 4) * 2 + (zh + d // 2) % 2
-        block = r.held[side, mixes[side].slot(d, step)]
-        behind = (z + 4 - group // 2) % 4
-        first = behind * 4 + (group % 2) * 2
+        groups = [((y + step) % 4) * 2 + (zh + d // 2) % 2 for step in range(4)]
+        slots = [mixes[side].slot(d, step) for step in range(4)]
+        block = jnp.concatenate([r.held[side, slot] for slot in slots], axis=1)
         rows_in = slice(side * 128, side * 128 + 128)
-        matrix = jnp.concatenate(
-            [r.columns[(j % 2) * 16 + first + j // 2, rows_in, :] for j in range(4)], axis=1
-        )
-        r.result[rows, :] += dot(block, matrix)
-        lanes = pl.ds(pl.multiple_of(group * 256 + side * 128, 128), 128)
-        r.low[rows, :] += dot_nt(block, r.down_o[:, lanes])
-
-    w0, w1 = weights
+        matrix = []
+        down = []
+        for group in groups:
+            first = ((z + 4 - group // 2) % 4) * 4 + (group % 2) * 2
+            matrix.append(
+                jnp.concatenate(
+                    [r.columns[(j % 2) * 16 + first + j // 2, rows_in, :] for j in range(4)],
+                    axis=1,
+                )
+            )
+            lanes = pl.ds(pl.multiple_of(group * 256 + side * 128, 128), 128)
+            down.append(r.down_here[:, lanes])
+        r.result[rows, :] += dot(block, jnp.concatenate(matrix, axis=0))
+        r.low[rows, :] += dot_nt(block, jnp.concatenate(down, axis=1))
+
+    w0, w1, w2 = weights
     k0, k1 = keys
     m0, m1 = mixes
     to_planes(w0)
-    w0.push_own(0)
-    w0.hand(0, 0)
+    for ring in weights:
+        ring.push_own(0)
+        ring.hand(0, 0)
+    normalize(1)
+    w0.from_left(0)
+    w0.from_right(0)
+    to_planes(w1)
+    w0.own(1)
+    normalize(2)
+    w0.own(2)
+    w1.from_left(0)
+    w1.from_right(0)
+    w0.own(3)
+    to_planes(w2)
+    normalize(3)
+    w0.from_left(1)
+    w0.from_right(1)
+    w0.from_left(2)
+    w0.from_right(2)
+    for copy in loads[10:]:
+        copy.wait()
+    reduced()
+    w0.from_left(3)
+    w0.from_right(3)
+    w2.from_left(0)
+    w2.from_right(0)
+    for d in range(1, 4):
+        w1.own(d)
 
     @pl.when(jnp.logical_not(stays))
     def _():
@@ -503,117 +524,89 @@
     @pl.when(stays)
     def _():
         copy = pltpu.make_async_copy(
-            r.wo, r.columns.at[(turn_seq % 2) * 16 + (turn_seq // 2) % 4], r.load.at[14]
+            r.wo, r.columns.at[(turn_seq % 2) * 16 + (turn_seq // 2) % 4], r.load.at[22]
         )
         copy.start()
         copy.wait()
 
-    normalize(0)
-    normalize(1)
-    w0.own(1)
-    w0.from_left(0)
-    w0.from_right(0)
-    normalize(2)
-    normalize(3)
-    w0.own(2)
-    for copy in loads[4:]:
-        copy.wait()
-    reduced()
-    w0.from_left(1)
-    w0.from_right(1)
-    w0.own(3)
-    w0.across(0)
-    accumulate(0, 0)
-    to_planes(w1)
-    w0.from_left(2)
-    w0.from_right(2)
-    w0.across(1)
-    accumulate(0, 1)
-    w0.from_left(3)
-    w0.from_right(3)
-    w1.push_own(0)
-    w1.hand(0, 0)
-    w1.own(1)
-    w0.across(2)
-    accumulate(0, 2)
-    w1.own(2)
-    w1.own(3)
-    w0.across(3)
-    accumulate(0, 3)
-    project(0)
-
-    for d in range(2):
+    for d in range(4):
+        w0.across(d)
+        accumulate(0, d)
+    project_keys(0)
+    for d in range(1, 4):
         w1.from_left(d)
         w1.from_right(d)
-    w1.across(0)
-    accumulate(1, 0)
-    for d in range(2, 4):
-        w1.from_left(d)
-        w1.from_right(d)
-    w1.across(1)
-    accumulate(1, 1)
+    for d in range(1, 4):
+        w2.own(d)
     k0.from_left(0)
     k0.from_right(1)
-    w1.across(2)
-    accumulate(1, 2)
-    w1.across(3)
-    accumulate(1, 3)
-    project(1)
+    for d in range(4):
+        w1.across(d)
+        accumulate(1, d)
     k0.from_left(1)
     k0.from_right(0)
     k0.own(2)
     k0.own(3)
+    for d in range(1, 4):
+        w2.from_left(d)
+        w2.from_right(d)
+    pass_on(0, 0)
+    pass_on(0, 1)
+    project_keys(1)
+
+    @pl.when(jnp.logical_not(stays))
+    def _():
+        columns.arrived(0, 0)
+
+    columns.hand(0, 0)
+    to_planes(columns)
+    for d in range(4):
+        w2.across(d)
+        accumulate(2, d)
+    project_queries(0)
+    project_queries(1)
+
     diagonal(0)
     near(0)
     own_plane(0, 3)
-    pass_on(0, 0)
-    pass_on(0, 1)
+    own_plane(0, 1)
+    own_plane(0, 2)
+    plane_before(0, 0)
     k1.from_left(0)
     k1.from_right(1)
-    own_plane(0, 1)
-    plane_before(0, 0)
-    own_plane(0, 2)
-    k1.from_left(1)
-    k1.from_right(0)
-    k1.own(2)
-    k1.own(3)
     for d in range(2, 4):
         k0.from_left(d, False)
         k0.from_right(d, False)
     plane_before(0, 3)
     plane_before(0, 1)
+    k1.from_left(1)
+    k1.from_right(0)
+    k1.own(2)
+    k1.own(3)
+    k0.across(2)
+    k0.across(3)
     pass_on(1, 0)
     pass_on(1, 1)
-    k0.across(2)
-    k0.across(3)
+    columns.push_own(0)
+    for d in range(1, 4):
+        columns.own(d)
     plane_before(0, 2)
     close(0)
 
-    @pl.when(jnp.logical_not(stays))
-    def _():
-        columns.arrived(0, 0)
-
-    to_planes(columns)
-    columns.hand(0, 0)
     diagonal(1)
     near(1)
     own_plane(1, 3)
     own_plane(1, 1)
-    for d in range(2):
-        m0.from_left(d)
-        m0.from_right(d)
     own_plane(1, 2)
     plane_before(1, 0)
-    columns.push_own(0)
-    for d in range(1, 4):
-        columns.own(d)
     for d in range(2, 4):
         k1.from_left(d, False)
         k1.from_right(d, False)
-    m0.own(2)
-    m0.own(3)
     plane_before(1, 3)
     plane_before(1, 1)
+    for d in range(2, 4):
+        m0.arrived(d, 0)
+        push_mixed(0, d)
     k1.across(2)
     k1.across(3)
     plane_before(1, 2)
@@ -622,41 +615,24 @@
     for d in range(4):
         columns.from_left(d)
         columns.from_right(d)
+    r.result[...] = jnp.zeros_like(r.result)
+    r.low[...] = jnp.zeros_like(r.low)
     for d in range(2, 4):
-        m0.from_left(d)
-        m0.from_right(d)
-    for d in range(2):
-        m1.from_left(d)
-        m1.from_right(d)
+        m1.arrived(d, 0)
+        push_mixed(1, d)
     for d in range(4):
         columns.across(d)
-    r.result[...] = jnp.zeros_like(r.result)
-    r.low[...] = jnp.zeros_like(r.low)
-    for d in range(4):
-        m0.across(d)
-    m1.own(2)
-    m1.own(3)
     for d in range(4):
         for step in range(4):
             columns.handed(d, step)
     for d in range(4):
-        for step in range(4):
-            add(0, d, step)
-    for d in range(2):
-        for step in (0, 1, 3):
-            add(1, d, step)
-    for d in range(2, 4):
-        m1.from_left(d)
-        m1.from_right(d)
-    for d in range(2):
-        m1.across(d)
-        add(1, d, 2)
-    for d in range(2, 4):
-        for step in (0, 1, 3):
-            add(1, d, step)
-    for d in range(2, 4):
-        m1.across(d)
-        add(1, d, 2)
+        for step in range(1, 4):
+            m0.arrived(d, step)
+        add(0, d)
+    for d in range(4):
+        for step in range(1, 4):
+            m1.arrived(d, step)
+        add(1, d)
     r.out[...] = (
         r.result[...] + ADAPTER_SCALING * dot(r.low[...].astype(BF16), r.up_here[...])
     ).astype(BF16)
@@ -708,19 +684,19 @@
         act=(activations, ANY),
         gain=(norm_gain.reshape(1, D), VMEM),
         shifted=(shifted, SMEM),
-        wq=(query_weight, VMEM),
-        wk=(key_weight, VMEM),
-        wv=(value_weight, VMEM),
-        wo=(output_weight, VMEM),
+        wq=(query_weight, ANY),
+        wk=(key_weight, ANY),
+        wv=(value_weight, ANY),
+        wo=(output_weight, ANY),
         down_q=(query_down.T, ANY),
         up_q=(query_up, ANY),
         down_k=(key_down.T, ANY),
         up_k=(key_up, ANY),
         down_v=(value_down.T, ANY),
         up_v=(value_up, ANY),
-        down_o=(output_down.T, VMEM),
+        down_o=(output_down.T, ANY),
         up_o=(output_up_matrix, ANY),
-        tables=(jnp.asarray(tables), VMEM),
+        tables=(jnp.asarray(tables), ANY),
         bases=(jnp.asarray(bases), VMEM),
     )
     out, sums = pl.pallas_call(

time: 132 us -> 118 us (0.89)
  Pallas kernels: 128 us -> 114 us
    pallas_call x1, Pallas kernels: 128 us -> 114 us  [body(): pl.pallas_call(kernel, out_shape=(jax.ShapeDtypeStruct((TOK, 512), BF16),...]
where the time goes in v3:
time: 118 us
  Pallas kernels  114 us (97%)
  local copies, waits for them, and re-layouts  3.13 us (3%)
    pallas_call x1, Pallas kernels, body(): pl.pallas_call(kernel, out_shape=(jax.ShapeDtypeStruct((TOK, 512), BF16),...  114 us
    unnamed x2, local copies, waits for them, and re-layouts  3.13 us

profile of v3, /device:TPU:38, one launch (start us, length us, event | category | flops | bytes accessed | tf_op | source)
XLA Modules:
  0.0 117.7 jit_solution(8320748909486402496)
XLA Ops:
  0.6 113.9 %shard_map.176 = (bf16[512,512]{1,0:T(8,128)(2,1)}, f32[2,512]{1,0:T(2,128)}) custom-call(bf16[512,4096]{1,0:T(8,128)(2,1)} %refs_0_.1, f32[1,4096]{1,0:T(1,128)} %bitcast.10, s32[16]{0:T(128)} %refs_2_.1, bf16[128,256]{1,0:T(8,128)(2,1)} %refs_3_.1, bf16[128,256]{1,0:T(8,128)(2,1)} %refs_4_.1, bf16[128,256]{1,0:T(8,128)(2,1)} %refs_5_.1, ...), custom_call_target="tpu_custom_call" | custom-call | tf_op jit(solution)/shard_map/pallas_call | solution.py:702
  114.6 1.9 %copy.21 = bf16[512,512]{1,0:T(8,128)(2,1)} copy(bf16[512,512]{1,0:T(8,128)(2,1)} %get-tuple-element.8) | data formatting | bytes 1048576
  116.5 1.3 %copy.22 = f32[512,2]{0,1:T(2,128)} copy(f32[512,2]{0,1:T(2,128)} %bitcast.11) | data formatting | bytes 8192

commit v4 on v3

--- a/solution.py
+++ b/solution.py
@@ -662,6 +662,11 @@
 SMEM = pl.BlockSpec(memory_space=pltpu.SMEM)
 
 
+def pass_through(out, sums, out_copy, sums_copy):
+    out_copy[...] = out[...]
+    sums_copy[...] = sums[...]
+
+
 def body(
     activations,
     norm_gain,
@@ -712,6 +717,15 @@
             collective_id=1, has_side_effects=True, vmem_limit_bytes=VMEM_BYTES
         ),
     )(*[arguments[name][0] for name in INPUTS])
+    out, sums = pl.pallas_call(
+        pass_through,
+        out_shape=(
+            jax.ShapeDtypeStruct((TOK, 512), BF16),
+            jax.ShapeDtypeStruct((2, TOK), F32),
+        ),
+        in_specs=[VMEM, VMEM],
+        out_specs=(VMEM, VMEM),
+    )(out, sums)
     return out, sums.T
 
 

time: 118 us -> 117 us (level)
  local copies, waits for them, and re-layouts: 3.13 us -> 0 us
  Pallas kernels: 114 us -> 116 us
    unnamed x2 -> x0, local copies, waits for them, and re-layouts: 3.13 us -> none
    pallas_call x0 -> x1, Pallas kernels: none -> 1.87 us  [body(): pl.pallas_call(pass_through, out_shape=(jax.ShapeDtypeStruct((TOK, 512),...]
where the time goes in v4:
time: 117 us; the launch traced here: 116 us
  Pallas kernels  116 us (99%)
    pallas_call x1, Pallas kernels, body(): pl.pallas_call(kernel, out_shape=(jax.ShapeDtypeStruct((TOK, 512), BF16),...  114 us

profile of v4, /device:TPU:38, one launch (start us, length us, event | category | flops | bytes accessed | tf_op | source)
XLA Modules:
  0.0 116.5 jit_solution(6577382421342768340)
XLA Ops:
  0.6 113.9 %shard_map.176 = (bf16[512,512]{1,0:T(8,128)(2,1)}, f32[2,512]{1,0:T(2,128)}) custom-call(bf16[512,4096]{1,0:T(8,128)(2,1)} %refs_0_.1, f32[1,4096]{1,0:T(1,128)} %bitcast.10, s32[16]{0:T(128)} %refs_2_.1, bf16[128,256]{1,0:T(8,128)(2,1)} %refs_3_.1, bf16[128,256]{1,0:T(8,128)(2,1)} %refs_4_.1, bf16[128,256]{1,0:T(8,128)(2,1)} %refs_5_.1, ...), custom_call_target="tpu_custom_call" | custom-call | tf_op jit(solution)/shard_map/pallas_call | solution.py:707
  114.6 1.9 %shard_map.177 = (bf16[512,512]{1,0:T(8,128)(2,1)}, f32[2,512]{1,0:T(2,128)}) custom-call(bf16[512,512]{1,0:T(8,128)(2,1)} %get-tuple-element.6.out, f32[2,512]{1,0:T(2,128)} %get-tuple-element.7.sums), custom_call_target="tpu_custom_call" | custom-call | tf_op jit(solution)/shard_map/pallas_call | solution.py:720
